TPU v7x, 32 devices: a whole 2x2x4 slice. The times are simulated.
32 devices in a mesh: gx: 4 (over y, core), gy: 2 (over x), gz: 4 (over z).
Axes of the slice: x: 2, y: 2, z: 4, core: 2. Of those that a mesh axis runs over, the one named last changes fastest.
Arguments:
- rhs: float32 [16, 8, 128, 512], P('gx', 'gy', 'gz'), may hold values from -6 to 6
- coef: float32 [16, 8, 128], P('gx', 'gy', 'gz'), may hold values from 1 to 4
- mass: float32 [512, 512], replicated, as said below
- smoother: float32 [512, 512], replicated, as said below
- lift: float32 [384, 512], replicated, may hold values from -0.15 to 0.15
- restrict: float32 [512, 8], replicated, may hold values from -0.25 to 0.25
- coarse_block_matrix: float32 [8, 8], replicated
- element_cluster_index: int32 [16, 8, 128], P('gx', 'gy', 'gz'), may hold values from 0 to 63
Outputs:
- corrected: float32 [16, 8, 128, 512], P('gx', 'gy', 'gz')
Inputs may be any that keep to these rules, and one draw needn't show every extreme that they name: `element_cluster_index`: index of an agglomerate within the element's own device block. `mass`: identity plus independent entries of deviation 0.15 / sqrt(512). `smoother`: identity minus the off-diagonal part of mass.
All inputs are finite; a program needn't handle non-finite values.
Results may differ from a plain program's by a relative error of at most 0.00005.
Values sent between devices are 32-bit elements; how exact they have to be, the bound alone decides.
No kernel may reach another device: no remote copies, remote signals or barrier semaphores. Data moves between devices by JAX's collectives and lax.ppermute only.
A program may use at most 64 MiB of HBM per device.

v0:
```python
import jax
import jax.numpy as jnp
from jax import lax
from jax.sharding import PartitionSpec as P

EDGE = 8
ELEMENT_DOFS = 512
FACE = 64
COARSE = 8
DEVICE_CLUSTERS = 64


def extended(cells, sides, width):
    for axis, dim in sides:
        count = lax.axis_size(axis)
        ends = count - 1
        head = lax.slice_in_dim(cells, 0, width, axis=dim)
        tail = lax.slice_in_dim(cells, cells.shape[dim] - width, cells.shape[dim], axis=dim)
        cells = jnp.concatenate(
            [
                lax.ppermute(tail, axis, [(i, (i + 1) % count) for i in range(ends)]),
                cells,
                lax.ppermute(head, axis, [((i + 1) % count, i) for i in range(ends)]),
            ],
            axis=dim,
        )
    return cells


def face_traces(field):
    cube = field.reshape(field.shape[:-1] + (EDGE, EDGE, EDGE))
    lead = field.shape[:-1]
    last = EDGE - 1
    parts = [
        cube[..., 0, :, :],
        cube[..., last, :, :],
        cube[..., :, 0, :],
        cube[..., :, last, :],
        cube[..., :, :, 0],
        cube[..., :, :, last],
    ]
    return jnp.concatenate([p.reshape(lead + (FACE,)) for p in parts], -1)


def neighbour_faces(padded):
    width = FACE
    return jnp.concatenate(
        [
            padded[:-2, 1:-1, 1:-1, width : 2 * width],
            padded[2:, 1:-1, 1:-1, 0:width],
            padded[1:-1, :-2, 1:-1, 3 * width : 4 * width],
            padded[1:-1, 2:, 1:-1, 2 * width : 3 * width],
            padded[1:-1, 1:-1, :-2, 5 * width : 6 * width],
            padded[1:-1, 1:-1, 2:, 4 * width : 5 * width],
        ],
        -1,
    )


def shards(rhs, coef, mass, smoother, lift, restrict, coarse_block_matrix, element_cluster_index):
    high = lax.Precision.HIGHEST

    def mult(a, b):
        return jnp.matmul(a, b, precision=high)

    def operate(field):
        padded = extended(face_traces(field), (("gx", 0), ("gy", 1), ("gz", 2)), 1)
        faces = neighbour_faces(padded)
        return coef[..., None] * mult(field, mass) - mult(faces, lift)

    first = mult(rhs, smoother) / coef[..., None]
    second = first + mult(rhs - operate(first), smoother) / coef[..., None]
    resid = rhs - operate(second)
    small = mult(resid.reshape(-1, ELEMENT_DOFS), restrict)
    labels = element_cluster_index.reshape(-1)
    onehot = (labels[:, None] == jnp.arange(DEVICE_CLUSTERS, dtype=jnp.int32)[None, :]).astype(
        jnp.float32
    )
    local_rhs = mult(small.T, onehot)
    counts = jnp.sum(onehot, 0)[None, :]
    coarse_rhs, column_counts = (
        lax.all_gather(local_rhs, "gx", axis=1, tiled=True),
        lax.all_gather(counts, "gx", axis=1, tiled=True),
    )
    weight_factor = 1.0 + column_counts
    zone = coarse_rhs / weight_factor
    zpad = extended(zone[None, None], (("gy", 0), ("gz", 1)), 1)
    nearby = zpad[0, 1] + zpad[2, 1] + zpad[1, 0] + zpad[1, 2]
    blocks_along = zone.shape[1] // DEVICE_CLUSTERS
    line_sum = jnp.sum(zone.reshape(COARSE, blocks_along, DEVICE_CLUSTERS), 1, keepdims=True)
    line_sum = jnp.broadcast_to(line_sum, (COARSE, blocks_along, DEVICE_CLUSTERS)).reshape(
        zone.shape
    )
    applied = weight_factor * mult(coarse_block_matrix, zone) - nearby - line_sum
    ztwo = zone + (coarse_rhs - applied) / weight_factor
    mine = lax.dynamic_slice_in_dim(
        ztwo, lax.axis_index("gx") * DEVICE_CLUSTERS, DEVICE_CLUSTERS, 1
    )
    corr = mult(mult(onehot, mine.T), restrict.T)
    return second + corr.reshape(second.shape)


def solution(mesh):
    return jax.shard_map(
        shards,
        mesh=mesh,
        in_specs=(
            P("gx", "gy", "gz", None),
            P("gx", "gy", "gz"),
            P(),
            P(),
            P(),
            P(),
            P(),
            P("gx", "gy", "gz"),
        ),
        out_specs=P("gx", "gy", "gz", None),
        check_vma=False,
    )
```

profile of v0, /device:TPU:0, one launch (start us, length us, event | category | flops | bytes accessed | tf_op | source)
XLA Modules:
  0.0 159.1 jit_solution(9057670267922510145)
XLA Ops:
  0.0 1.2 copy-done
  1.2 3.1 %convolution_divide_fusion.1 = f32[4,4,32,512]{3,2,1,0:T(8,128)S(1)} fusion(f32[4,4,32,512]{3,2,1,0:T(8,128)} %param.8, f32[512,512]{1,0:T(8,128)S(1)} %copy-done, f32[4,4,32]{2,1,0:T(4,128)} %param.9), kind=kOutput, calls=%fused_computation.7 | convolution fusion | flops 1610874880 | bytes 3147776 | tf_op jit(solution)/shard_map/dot_general | solution.py:64
  4.3 2.7 %copy.33 = f32[4,4,32,512]{2,3,1,0:T(8,128)} copy(f32[4,4,32,512]{3,2,1,0:T(8,128)S(1)} %convolution_divide_fusion.1) | data formatting | bytes 2097152 | tf_op jit(solution)/shard_map/div | solution.py:71
  7.0 2.1 %slice_bitcast_fusion.6 = (f32[4,4,32,64]{2,3,1,0:T(8,128)S(1)}, f32[4,4,32,64]{2,3,1,0:T(8,128)}) fusion(f32[4,4,32,8,8,8]{2,5,4,3,1,0:T(8,128)} %bitcast.77), kind=kLoop, calls=%fused_computation.25 | loop fusion | bytes 524288 | tf_op jit(solution)/shard_map/reshape;squeeze | solution.py:42
  9.1 2.3 %slice_bitcast_fusion.4 = (f32[4,4,32,64]{2,3,1,0:T(8,128)}, f32[4,4,32,64]{2,3,1,0:T(8,128)}) fusion(f32[4,4,32,8,8,8]{2,5,4,3,1,0:T(8,128)} %bitcast.78), kind=kLoop, calls=%fused_computation.23 | loop fusion | bytes 524288 | tf_op jit(solution)/shard_map/reshape;squeeze | solution.py:42
  11.5 5.4 %fusion.21 = (f32[4,4,32,8,8,1]{2,5,4,3,1,0:T(1,128)S(1)}, f32[4,4,32,8,8,1]{2,5,4,3,1,0:T(1,128)}) fusion(f32[4,4,32,8,8,8]{2,5,4,3,1,0:T(8,128)} %bitcast.79), kind=kLoop, calls=%fused_computation.99 | loop fusion | bytes 524288 | tf_op jit(solution)/shard_map/slice | solution.py:40
  16.9 2.0 %copy.34 = f32[4,4,32,64]{3,2,1,0:T(8,128)} copy(f32[4,4,32,64]{2,3,1,0:T(8,128)} %get-tuple-element.16) | data formatting | bytes 262144 | tf_op jit(solution)/shard_map/reshape;squeeze | solution.py:42
  18.9 0.9 copy.35
  19.8 2.0 %copy.36 = f32[4,4,32,64]{3,2,1,0:T(8,128)} copy(f32[4,4,32,64]{2,3,1,0:T(8,128)} %get-tuple-element.14) | data formatting | bytes 262144 | tf_op jit(solution)/shard_map/reshape;squeeze | solution.py:42
  21.8 2.0 %copy.37 = f32[4,4,32,64]{3,2,1,0:T(8,128)} copy(f32[4,4,32,64]{2,3,1,0:T(8,128)} %get-tuple-element.13) | data formatting | bytes 262144 | tf_op jit(solution)/shard_map/reshape;squeeze | solution.py:42
  23.7 1.9 %copy.38 = f32[4,4,32,64]{3,2,1,0:T(8,128)} copy(f32[4,4,32,64]{2,3,1,0:T(8,128)} %bitcast.87) | data formatting | bytes 262144 | tf_op jit(solution)/shard_map/reshape;squeeze | solution.py:42
  25.7 0.9 copy.39
  26.6 1.7 %concatenate.65 = f32[4,4,32,384]{3,2,1,0:T(8,128)S(1)} concatenate(f32[4,4,32,64]{3,2,1,0:T(8,128)} %copy.34, f32[4,4,32,64]{3,2,1,0:T(8,128)} %copy.35, f32[4,4,32,64]{3,2,1,0:T(8,128)} %copy.36, f32[4,4,32,64]{3,2,1,0:T(8,128)} %copy.37, f32[4,4,32,64]{3,2,1,0:T(8,128)} %copy.38, f32[4,4,32,64]{3,2,1,0:T(8,128)} %copy.39), dimensions={3} | concatenate | bytes 1572864 | tf_op jit(solution)/shard_map/concatenate | solution.py:42
  28.3 0.7 fusion.23
  29.0 2.4 %collective-permute-start = (f32[1,4,32,384]{3,2,1,0:T(8,128)}, f32[1,4,32,384]{3,2,1,0:T(8,128)S(1)}, u32[]{:S(2)}, u32[]{:S(2)}) collective-permute-start(f32[1,4,32,384]{3,2,1,0:T(8,128)} %get-tuple-element.40), channel_id=1, source_target_pairs={{0,8},{8,16},{16,24},{1,9},{9,17},{17,25},{2,10},{10,18},{18,26},{... | collective-permute-start | bytes 589832 | tf_op jit(solution)/shard_map/ppermute | solution.py:21
  31.3 1.3 collective-permute-start.1
  32.7 0.6 dynamic-slice
  34.3 8.9 %all-reduce = f32[256]{0:T(256)S(1)} all-reduce(f32[256]{0:T(256)S(1)} %dynamic-update-slice), channel_id=2, replica_groups=mesh['gx'=4,'gy'=2,'gz'=4] {'gx'}, use_global_device_ids=true, to_apply=%add | all-reduce | flops 256 | bytes 2048
  43.2 1.3 collective-permute-start.3
  44.5 4.6 %collective-permute-start.2 = (f32[6,1,32,384]{3,2,1,0:T(8,128)S(1)}, f32[6,1,32,384]{3,2,1,0:T(8,128)S(1)}, u32[]{:S(2)}, u32[]{:S(2)}) collective-permute-start(f32[6,1,32,384]{3,2,1,0:T(8,128)S(1)} %get-tuple-element.30), channel_id=1, source_target_pairs={{0,4},{1,5},{2,6},{3,7},{8,12},{9,13},{10,14},{11,15},{16,20},{17,... | collective-permute-start | bytes 884744 | tf_op jit(solution)/shard_map/ppermute | solution.py:21
  49.2 4.0 %convolution_multiply_fusion.1 = f32[4,4,32,512]{3,2,1,0:T(8,128)} fusion(f32[4,4,32,512]{3,2,1,0:T(8,128)} %copy-done.2, f32[512,512]{1,0:T(8,128)S(1)} %copy-done.1, f32[4,4,32]{2,1,0:T(4,128)S(1)} %copy-done.5), kind=kOutput, calls=%fused_computation.6 | convolution fusion | flops 1610874880 | bytes 3147776 | tf_op jit(solution)/shard_map/dot_general | solution.py:64
  53.2 0.7 collective-permute-done.3
  53.9 1.2 collective-permute-done.2
  55.2 3.5 %collective-permute-start.4 = (f32[6,6,1,384]{3,2,1,0:T(1,128)S(1)}, f32[6,6,1,384]{3,2,1,0:T(1,128)S(1)}, u32[]{:S(2)}, u32[]{:S(2)}) collective-permute-start(f32[6,6,1,384]{3,2,1,0:T(1,128)S(1)} %get-tuple-element.24), channel_id=1, source_target_pairs={{0,1},{1,2},{2,3},{4,5},{5,6},{6,7},{8,9},{9,10},{10,11},{12,13},{... | collective-permute-start | bytes 165896 | tf_op jit(solution)/shard_map/ppermute | solution.py:21
  58.7 1.5 collective-permute-start.5
  60.2 0.8 pad_maximum_fusion.34
  60.9 3.8 %collective-permute-done.5 = f32[6,6,1,384]{3,2,1,0:T(1,128)S(1)} collective-permute-done((f32[6,6,1,384]{3,2,1,0:T(1,128)S(1)}, f32[6,6,1,384]{3,2,1,0:T(1,128)S(1)}, u32[]{:S(2)}, u32[]{:S(2)}) %collective-permute-start.5) | collective-permute-done | bytes 55328 | tf_op jit(solution)/shard_map/ppermute | solution.py:23
  64.7 1.2 pad_maximum_fusion.24
  66.0 1.6 %concatenate.74 = f32[4,4,32,384]{3,2,1,0:T(8,128)S(1)} concatenate(f32[4,4,32,64]{3,2,1,0:T(8,128)} %get-tuple-element.34, f32[4,4,32,64]{3,2,1,0:T(8,128)} %get-tuple-element.36, f32[4,4,32,64]{3,2,1,0:T(8,128)} %get-tuple-element.26, f32[4,4,32,64]{3,2,1,0:T(8,128)S(1)} %get-tuple-element.35, f32[4,4,32,64]{3,2,1,0:T(8,128)} %get-tuple-element.22, ...), dimensions={3} | concatenate | bytes 1572864 | tf_op jit(solution)/shard_map/concatenate | solution.py:47
  67.6 3.4 %fusion.2 = f32[4,4,32,512]{3,2,1,0:T(8,128)S(1)} fusion(f32[4,4,32,512]{3,2,1,0:T(8,128)} %param.8, f32[4,4,32,512]{3,2,1,0:T(8,128)S(1)} %copy-done.3, f32[4,4,32,384]{3,2,1,0:T(8,128)S(1)} %concatenate.74, f32[384,512]{1,0:T(8,128)} %param.12), kind=kOutput, calls=%fused_computation.8 | convolution fusion | flops 1208483840 | bytes 4718592 | tf_op jit(solution)/shard_map/dot_general | solution.py:64
  71.0 3.1 %fusion.1 = f32[4,4,32,512]{3,2,1,0:T(8,128)S(1)} fusion(f32[4,4,32,512]{3,2,1,0:T(8,128)} %copy-done.2, f32[4,4,32,512]{3,2,1,0:T(8,128)S(1)} %fusion.2, f32[512,512]{1,0:T(8,128)S(1)} %copy-done, f32[4,4,32]{2,1,0:T(4,128)S(1)} %copy-done.5), kind=kOutput, calls=%fused_computation.5 | convolution fusion | flops 1611137024 | bytes 4196352 | tf_op jit(solution)/shard_map/dot_general | solution.py:64
  74.1 2.7 %copy.40 = f32[4,4,32,512]{2,3,1,0:T(8,128)} copy(f32[4,4,32,512]{3,2,1,0:T(8,128)S(1)} %fusion.1) | data formatting | bytes 2097152 | tf_op jit(solution)/shard_map/add | solution.py:72
  76.7 2.3 %slice_bitcast_fusion.2 = (f32[4,4,32,64]{2,3,1,0:T(8,128)}, f32[4,4,32,64]{2,3,1,0:T(8,128)}) fusion(f32[4,4,32,8,8,8]{2,5,4,3,1,0:T(8,128)} %bitcast.80), kind=kLoop, calls=%fused_computation.21 | loop fusion | bytes 524288 | tf_op jit(solution)/shard_map/reshape;squeeze | solution.py:42
  79.0 2.3 %slice_bitcast_fusion = (f32[4,4,32,64]{2,3,1,0:T(8,128)}, f32[4,4,32,64]{2,3,1,0:T(8,128)}) fusion(f32[4,4,32,8,8,8]{2,5,4,3,1,0:T(8,128)} %bitcast.81), kind=kLoop, calls=%fused_computation.19 | loop fusion | bytes 524288 | tf_op jit(solution)/shard_map/reshape;squeeze | solution.py:42
  81.4 4.6 %fusion.20 = (f32[4,4,32,8,8,1]{2,5,4,3,1,0:T(1,128)S(1)}, f32[4,4,32,8,8,1]{2,5,4,3,1,0:T(1,128)S(1)}) fusion(f32[4,4,32,8,8,8]{2,5,4,3,1,0:T(8,128)} %bitcast.82), kind=kLoop, calls=%fused_computation.98 | loop fusion | bytes 524288 | tf_op jit(solution)/shard_map/slice | solution.py:40
  86.0 1.9 %copy.41 = f32[4,4,32,64]{3,2,1,0:T(8,128)} copy(f32[4,4,32,64]{2,3,1,0:T(8,128)} %get-tuple-element.10) | data formatting | bytes 262144 | tf_op jit(solution)/shard_map/reshape;squeeze | solution.py:42
  87.9 1.9 %copy.42 = f32[4,4,32,64]{3,2,1,0:T(8,128)} copy(f32[4,4,32,64]{2,3,1,0:T(8,128)} %get-tuple-element.9) | data formatting | bytes 262144 | tf_op jit(solution)/shard_map/reshape;squeeze | solution.py:42
  89.8 1.9 %copy.43 = f32[4,4,32,64]{3,2,1,0:T(8,128)} copy(f32[4,4,32,64]{2,3,1,0:T(8,128)} %get-tuple-element.8) | data formatting | bytes 262144 | tf_op jit(solution)/shard_map/reshape;squeeze | solution.py:42
  91.8 1.9 %copy.44 = f32[4,4,32,64]{3,2,1,0:T(8,128)} copy(f32[4,4,32,64]{2,3,1,0:T(8,128)} %get-tuple-element.7) | data formatting | bytes 262144 | tf_op jit(solution)/shard_map/reshape;squeeze | solution.py:42
  93.7 0.9 copy.45
  94.8 1.6 %concatenate.75 = f32[4,4,32,384]{3,2,1,0:T(8,128)S(1)} concatenate(f32[4,4,32,64]{3,2,1,0:T(8,128)} %copy.41, f32[4,4,32,64]{3,2,1,0:T(8,128)} %copy.42, f32[4,4,32,64]{3,2,1,0:T(8,128)} %copy.43, f32[4,4,32,64]{3,2,1,0:T(8,128)} %copy.44, f32[4,4,32,64]{3,2,1,0:T(8,128)} %copy.45, f32[4,4,32,64]{3,2,1,0:T(8,128)S(1)} %copy.46), dimensions={3} | concatenate | bytes 1572864 | tf_op jit(solution)/shard_map/concatenate | solution.py:42
  96.5 1.3 collective-permute-start.6
  97.8 1.3 collective-permute-start.7
  99.2 3.8 %collective-permute-done.7 = f32[1,4,32,384]{3,2,1,0:T(8,128)S(1)} collective-permute-done((f32[1,4,32,384]{3,2,1,0:T(8,128)S(1)}, f32[1,4,32,384]{3,2,1,0:T(8,128)S(1)}, u32[]{:S(2)}, u32[]{:S(2)}) %collective-permute-start.7) | collective-permute-done | bytes 196640 | tf_op jit(solution)/shard_map/ppermute | solution.py:23
  103.0 1.3 collective-permute-start.9
  104.3 4.6 %collective-permute-start.8 = (f32[6,1,32,384]{3,2,1,0:T(8,128)S(1)}, f32[6,1,32,384]{3,2,1,0:T(8,128)S(1)}, u32[]{:S(2)}, u32[]{:S(2)}) collective-permute-start(f32[6,1,32,384]{3,2,1,0:T(8,128)S(1)} %get-tuple-element.28), channel_id=1, source_target_pairs={{0,4},{1,5},{2,6},{3,7},{8,12},{9,13},{10,14},{11,15},{16,20},{17,... | collective-permute-start | bytes 884744 | tf_op jit(solution)/shard_map/ppermute | solution.py:21
  108.9 4.0 %convolution_multiply_fusion = f32[4,4,32,512]{3,2,1,0:T(8,128)} fusion(f32[4,4,32,512]{3,2,1,0:T(8,128)S(1)} %fusion.1, f32[512,512]{1,0:T(8,128)} %param.10, f32[4,4,32]{2,1,0:T(4,128)S(1)} %copy-done.5), kind=kOutput, calls=%fused_computation.3 | convolution fusion | flops 1610874880 | bytes 3147776 | tf_op jit(solution)/shard_map/dot_general | solution.py:64
  113.2 3.5 %collective-permute-start.10 = (f32[6,6,1,384]{3,2,1,0:T(1,128)S(1)}, f32[6,6,1,384]{3,2,1,0:T(1,128)S(1)}, u32[]{:S(2)}, u32[]{:S(2)}) collective-permute-start(f32[6,6,1,384]{3,2,1,0:T(1,128)S(1)} %get-tuple-element.20), channel_id=1, source_target_pairs={{0,1},{1,2},{2,3},{4,5},{5,6},{6,7},{8,9},{9,10},{10,11},{12,13},{... | collective-permute-start | bytes 165896 | tf_op jit(solution)/shard_map/ppermute | solution.py:21
  116.7 1.3 collective-permute-start.11
  118.1 0.4 collective-permute-done.10
  118.5 4.3 %collective-permute-done.11 = f32[6,6,1,384]{3,2,1,0:T(1,128)S(1)} collective-permute-done((f32[6,6,1,384]{3,2,1,0:T(1,128)S(1)}, f32[6,6,1,384]{3,2,1,0:T(1,128)S(1)}, u32[]{:S(2)}, u32[]{:S(2)}) %collective-permute-start.11) | collective-permute-done | bytes 55328 | tf_op jit(solution)/shard_map/ppermute | solution.py:23
  122.7 1.2 pad_maximum_fusion.6
  124.0 1.6 concatenate.84
  125.6 3.6 %fusion.3 = f32[4,4,32,512]{3,2,1,0:T(8,128)S(1)} fusion(f32[4,4,32,512]{3,2,1,0:T(8,128)} %param.8, f32[4,4,32,512]{3,2,1,0:T(8,128)} %convolution_multiply_fusion, f32[4,4,32,384]{3,2,1,0:T(8,128)S(1)} %concatenate.84, f32[384,512]{1,0:T(8,128)} %param.12), kind=kOutput, calls=%fused_computation.9 | convolution fusion | flops 1208483840 | bytes 4718592 | tf_op jit(solution)/shard_map/dot_general | solution.py:64
  129.2 1.0 fusion.24
  130.3 7.2 %all-gather.1 = f32[4,64,8]{1,2,0:T(8,128)S(1)} all-gather(f32[1,64,8]{1,2,0:T(8,128)S(1)} %convolution_bitcast_fusion), channel_id=1, replica_groups=mesh['gx'=4,'gy'=2,'gz'=4] {'gx'}, dimensions={0}, use_global_device_ids=true | all-gather | bytes 10240 | tf_op jit(solution)/shard_map/all_gather | solution.py:82
  137.6 4.4 %collective-permute-start.12 = (f32[1,1,8,256]{3,2,1,0:T(8,128)S(1)}, f32[1,1,8,256]{3,2,1,0:T(8,128)S(1)}, u32[]{:S(2)}, u32[]{:S(2)}) collective-permute-start(f32[1,1,8,256]{3,2,1,0:T(8,128)S(1)} %fusion.40), channel_id=1, source_target_pairs={{0,4},{1,5},{2,6},{3,7},{8,12},{9,13},{10,14},{11,15},{16,20},{17,... | collective-permute-start | bytes 24584 | tf_op jit(solution)/shard_map/ppermute | solution.py:21
  142.0 1.3 collective-permute-start.13
  143.4 4.1 %collective-permute-done.13 = f32[1,1,8,256]{3,2,1,0:T(8,128)S(1)} collective-permute-done((f32[1,1,8,256]{3,2,1,0:T(8,128)S(1)}, f32[1,1,8,256]{3,2,1,0:T(8,128)S(1)}, u32[]{:S(2)}, u32[]{:S(2)}) %collective-permute-start.13) | collective-permute-done | bytes 8224 | tf_op jit(solution)/shard_map/ppermute | solution.py:23
  147.5 3.5 %collective-permute-start.14 = (f32[3,1,8,256]{3,2,1,0:T(8,128)S(1)}, f32[3,1,8,256]{3,2,1,0:T(8,128)S(1)}, u32[]{:S(2)}, u32[]{:S(2)}) collective-permute-start(f32[3,1,8,256]{3,2,1,0:T(8,128)S(1)} %pad_maximum_fusion.52), channel_id=1, source_target_pairs={{0,1},{1,2},{2,3},{4,5},{5,6},{6,7},{8,9},{9,10},{10,11},{12,13},{... | collective-permute-start | bytes 73736 | tf_op jit(solution)/shard_map/ppermute | solution.py:21
  151.0 1.3 collective-permute-start.15
  152.5 4.2 %collective-permute-done.15 = f32[3,1,8,256]{3,2,1,0:T(8,128)S(1)} collective-permute-done((f32[3,1,8,256]{3,2,1,0:T(8,128)S(1)}, f32[3,1,8,256]{3,2,1,0:T(8,128)S(1)}, u32[]{:S(2)}, u32[]{:S(2)}) %collective-permute-start.15) | collective-permute-done | bytes 24608 | tf_op jit(solution)/shard_map/ppermute | solution.py:23
  156.9 1.0 fusion.25
  158.0 1.2 add.41
  (50 shorter events, 2.0 us)
Async XLA Ops:
  0.0 1.2 copy-start
  4.3 7.2 %copy-start.2 = (f32[4,4,32,512]{3,2,1,0:T(8,128)}, f32[4,4,32,512]{3,2,1,0:T(8,128)S(1)}, u32[]{:S(2)}) copy-start(f32[4,4,32,512]{3,2,1,0:T(8,128)S(1)} %convolution_divide_fusion.1) | copy-start | bytes 3145732
  16.9 15.7 %copy-start.6 = (s32[4,4,32]{2,1,0:T(4,128)S(1)}, s32[4,4,32]{2,1,0:T(4,128)}, u32[]{:S(2)}) copy-start(s32[4,4,32]{2,1,0:T(4,128)} %param.15) | copy-start | bytes 6148
  16.9 15.8 %copy-start.8 = (u32[32]{0:T(128)S(1)}, u32[32]{0:T(128)}, u32[]{:S(2)}) copy-start(u32[32]{0:T(128)} %constant.17) | copy-start | bytes 388
  19.8 29.4 %copy-start.1 = (f32[512,512]{1,0:T(8,128)S(1)}, f32[512,512]{1,0:T(8,128)}, u32[]{:S(2)}) copy-start(f32[512,512]{1,0:T(8,128)} %param.10) | copy-start | bytes 3145732
  19.8 29.4 %copy-start.5 = (f32[4,4,32]{2,1,0:T(4,128)S(1)}, f32[4,4,32]{2,1,0:T(4,128)}, u32[]{:S(2)}) copy-start(f32[4,4,32]{2,1,0:T(4,128)} %param.9) | copy-start | bytes 6148
  29.0 14.2 %collective-permute-start = (f32[1,4,32,384]{3,2,1,0:T(8,128)}, f32[1,4,32,384]{3,2,1,0:T(8,128)S(1)}, u32[]{:S(2)}, u32[]{:S(2)}) collective-permute-start(f32[1,4,32,384]{3,2,1,0:T(8,128)} %get-tuple-element.40), channel_id=1, source_target_pairs={{0,8},{8,16},{16,24},{1,9},{9,17},{17,25},{2,10},{10,18},{18,26},{... | collective-permute-start | bytes 589832 | tf_op jit(solution)/shard_map/ppermute | solution.py:21
  31.3 11.9 %collective-permute-start.1 = (f32[1,4,32,384]{3,2,1,0:T(8,128)S(1)}, f32[1,4,32,384]{3,2,1,0:T(8,128)S(1)}, u32[]{:S(2)}, u32[]{:S(2)}) collective-permute-start(f32[1,4,32,384]{3,2,1,0:T(8,128)S(1)} %get-tuple-element.39), channel_id=1, source_target_pairs={{8,0},{16,8},{24,16},{9,1},{17,9},{25,17},{10,2},{18,10},{26,18},{... | collective-permute-start | bytes 589832 | tf_op jit(solution)/shard_map/ppermute | solution.py:23
  43.2 10.7 %collective-permute-start.3 = (f32[6,1,32,384]{3,2,1,0:T(8,128)S(1)}, f32[6,1,32,384]{3,2,1,0:T(8,128)S(1)}, u32[]{:S(2)}, u32[]{:S(2)}) collective-permute-start(f32[6,1,32,384]{3,2,1,0:T(8,128)S(1)} %get-tuple-element.29), channel_id=1, source_target_pairs={{4,0},{5,1},{6,2},{7,3},{12,8},{13,9},{14,10},{15,11},{20,16},{21,... | collective-permute-start | bytes 884744 | tf_op jit(solution)/shard_map/ppermute | solution.py:23
  44.5 10.6 %collective-permute-start.2 = (f32[6,1,32,384]{3,2,1,0:T(8,128)S(1)}, f32[6,1,32,384]{3,2,1,0:T(8,128)S(1)}, u32[]{:S(2)}, u32[]{:S(2)}) collective-permute-start(f32[6,1,32,384]{3,2,1,0:T(8,128)S(1)} %get-tuple-element.30), channel_id=1, source_target_pairs={{0,4},{1,5},{2,6},{3,7},{8,12},{9,13},{10,14},{11,15},{16,20},{17,... | collective-permute-start | bytes 884744 | tf_op jit(solution)/shard_map/ppermute | solution.py:21
  53.2 14.4 %copy-start.3 = (f32[4,4,32,512]{3,2,1,0:T(8,128)S(1)}, f32[4,4,32,512]{3,2,1,0:T(8,128)}, u32[]{:S(2)}) copy-start(f32[4,4,32,512]{3,2,1,0:T(8,128)} %convolution_multiply_fusion.1) | copy-start | bytes 3145732
  55.2 5.8 %collective-permute-start.4 = (f32[6,6,1,384]{3,2,1,0:T(1,128)S(1)}, f32[6,6,1,384]{3,2,1,0:T(1,128)S(1)}, u32[]{:S(2)}, u32[]{:S(2)}) collective-permute-start(f32[6,6,1,384]{3,2,1,0:T(1,128)S(1)} %get-tuple-element.24), channel_id=1, source_target_pairs={{0,1},{1,2},{2,3},{4,5},{5,6},{6,7},{8,9},{9,10},{10,11},{12,13},{... | collective-permute-start | bytes 165896 | tf_op jit(solution)/shard_map/ppermute | solution.py:21
  58.7 6.0 %collective-permute-start.5 = (f32[6,6,1,384]{3,2,1,0:T(1,128)S(1)}, f32[6,6,1,384]{3,2,1,0:T(1,128)S(1)}, u32[]{:S(2)}, u32[]{:S(2)}) collective-permute-start(f32[6,6,1,384]{3,2,1,0:T(1,128)S(1)} %get-tuple-element.23), channel_id=1, source_target_pairs={{1,0},{2,1},{3,2},{5,4},{6,5},{7,6},{9,8},{10,9},{11,10},{13,12},{... | collective-permute-start | bytes 165896 | tf_op jit(solution)/shard_map/ppermute | solution.py:23
  96.5 2.7 %collective-permute-start.6 = (f32[1,4,32,384]{3,2,1,0:T(8,128)S(1)}, f32[1,4,32,384]{3,2,1,0:T(8,128)S(1)}, u32[]{:S(2)}, u32[]{:S(2)}) collective-permute-start(f32[1,4,32,384]{3,2,1,0:T(8,128)S(1)} %get-tuple-element.38), channel_id=1, source_target_pairs={{0,8},{8,16},{16,24},{1,9},{9,17},{17,25},{2,10},{10,18},{18,26},{... | collective-permute-start | bytes 589832 | tf_op jit(solution)/shard_map/ppermute | solution.py:21
  97.8 5.2 %collective-permute-start.7 = (f32[1,4,32,384]{3,2,1,0:T(8,128)S(1)}, f32[1,4,32,384]{3,2,1,0:T(8,128)S(1)}, u32[]{:S(2)}, u32[]{:S(2)}) collective-permute-start(f32[1,4,32,384]{3,2,1,0:T(8,128)S(1)} %get-tuple-element.37), channel_id=1, source_target_pairs={{8,0},{16,8},{24,16},{9,1},{17,9},{25,17},{10,2},{18,10},{26,18},{... | collective-permute-start | bytes 589832 | tf_op jit(solution)/shard_map/ppermute | solution.py:23
  103.0 9.9 %collective-permute-start.9 = (f32[6,1,32,384]{3,2,1,0:T(8,128)S(1)}, f32[6,1,32,384]{3,2,1,0:T(8,128)S(1)}, u32[]{:S(2)}, u32[]{:S(2)}) collective-permute-start(f32[6,1,32,384]{3,2,1,0:T(8,128)S(1)} %get-tuple-element.27), channel_id=1, source_target_pairs={{4,0},{5,1},{6,2},{7,3},{12,8},{13,9},{14,10},{15,11},{20,16},{21,... | collective-permute-start | bytes 884744 | tf_op jit(solution)/shard_map/ppermute | solution.py:23
  104.3 8.8 %collective-permute-start.8 = (f32[6,1,32,384]{3,2,1,0:T(8,128)S(1)}, f32[6,1,32,384]{3,2,1,0:T(8,128)S(1)}, u32[]{:S(2)}, u32[]{:S(2)}) collective-permute-start(f32[6,1,32,384]{3,2,1,0:T(8,128)S(1)} %get-tuple-element.28), channel_id=1, source_target_pairs={{0,4},{1,5},{2,6},{3,7},{8,12},{9,13},{10,14},{11,15},{16,20},{17,... | collective-permute-start | bytes 884744 | tf_op jit(solution)/shard_map/ppermute | solution.py:21
  113.2 5.3 %collective-permute-start.10 = (f32[6,6,1,384]{3,2,1,0:T(1,128)S(1)}, f32[6,6,1,384]{3,2,1,0:T(1,128)S(1)}, u32[]{:S(2)}, u32[]{:S(2)}) collective-permute-start(f32[6,6,1,384]{3,2,1,0:T(1,128)S(1)} %get-tuple-element.20), channel_id=1, source_target_pairs={{0,1},{1,2},{2,3},{4,5},{5,6},{6,7},{8,9},{9,10},{10,11},{12,13},{... | collective-permute-start | bytes 165896 | tf_op jit(solution)/shard_map/ppermute | solution.py:21
  116.7 6.0 %collective-permute-start.11 = (f32[6,6,1,384]{3,2,1,0:T(1,128)S(1)}, f32[6,6,1,384]{3,2,1,0:T(1,128)S(1)}, u32[]{:S(2)}, u32[]{:S(2)}) collective-permute-start(f32[6,6,1,384]{3,2,1,0:T(1,128)S(1)} %get-tuple-element.19), channel_id=1, source_target_pairs={{1,0},{2,1},{3,2},{5,4},{6,5},{7,6},{9,8},{10,9},{11,10},{13,12},{... | collective-permute-start | bytes 165896 | tf_op jit(solution)/shard_map/ppermute | solution.py:23
  124.0 5.2 %copy-start.4 = (f32[512,8]{0,1:T(8,128)S(1)}, f32[512,8]{0,1:T(8,128)}, u32[]{:S(2)}) copy-start(f32[512,8]{0,1:T(8,128)} %param.13) | copy-start | bytes 49156
  124.0 28.3 %copy-start.7 = (f32[8,8]{1,0:T(8,128)S(1)}, f32[8,8]{1,0:T(8,128)}, u32[]{:S(2)}) copy-start(f32[8,8]{1,0:T(8,128)} %param.14) | copy-start | bytes 772
  137.6 5.8 %collective-permute-start.12 = (f32[1,1,8,256]{3,2,1,0:T(8,128)S(1)}, f32[1,1,8,256]{3,2,1,0:T(8,128)S(1)}, u32[]{:S(2)}, u32[]{:S(2)}) collective-permute-start(f32[1,1,8,256]{3,2,1,0:T(8,128)S(1)} %fusion.40), channel_id=1, source_target_pairs={{0,4},{1,5},{2,6},{3,7},{8,12},{9,13},{10,14},{11,15},{16,20},{17,... | collective-permute-start | bytes 24584 | tf_op jit(solution)/shard_map/ppermute | solution.py:21
  142.0 5.5 %collective-permute-start.13 = (f32[1,1,8,256]{3,2,1,0:T(8,128)S(1)}, f32[1,1,8,256]{3,2,1,0:T(8,128)S(1)}, u32[]{:S(2)}, u32[]{:S(2)}) collective-permute-start(f32[1,1,8,256]{3,2,1,0:T(8,128)S(1)} %fusion.40), channel_id=1, source_target_pairs={{4,0},{5,1},{6,2},{7,3},{12,8},{13,9},{14,10},{15,11},{20,16},{21,... | collective-permute-start | bytes 24584 | tf_op jit(solution)/shard_map/ppermute | solution.py:23
  147.5 5.0 %collective-permute-start.14 = (f32[3,1,8,256]{3,2,1,0:T(8,128)S(1)}, f32[3,1,8,256]{3,2,1,0:T(8,128)S(1)}, u32[]{:S(2)}, u32[]{:S(2)}) collective-permute-start(f32[3,1,8,256]{3,2,1,0:T(8,128)S(1)} %pad_maximum_fusion.52), channel_id=1, source_target_pairs={{0,1},{1,2},{2,3},{4,5},{5,6},{6,7},{8,9},{9,10},{10,11},{12,13},{... | collective-permute-start | bytes 73736 | tf_op jit(solution)/shard_map/ppermute | solution.py:21
  151.0 5.7 %collective-permute-start.15 = (f32[3,1,8,256]{3,2,1,0:T(8,128)S(1)}, f32[3,1,8,256]{3,2,1,0:T(8,128)S(1)}, u32[]{:S(2)}, u32[]{:S(2)}) collective-permute-start(f32[3,1,8,256]{3,2,1,0:T(8,128)S(1)} %pad_maximum_fusion.52), channel_id=1, source_target_pairs={{1,0},{2,1},{3,2},{5,4},{6,5},{7,6},{9,8},{10,9},{11,10},{13,12},{... | collective-permute-start | bytes 73736 | tf_op jit(solution)/shard_map/ppermute | solution.py:23
where the time goes:
time: 160 us; the launch traced here: 159 us
  local copies, waits for them, and re-layouts  52.7 us (33%)
  starting transfers between devices  38.1 us (24%)
  matrix products  23.7 us (15%)
  waiting for transfers between devices  22.7 us (14%)
  blocking collectives  16 us (10%)
  other arithmetic  4.87 us (3%)
    ppermute x8, starting transfers between devices, extended(): lax.ppermute(tail, axis, [(i, (i + 1) % count) for i in range(ends)])  27.6 us
    another operation x16, local copies, waits for them, and re-layouts, face_traces(): return jnp.concatenate([p.reshape(lead + (FACE,)) for p in parts], -1)  27.6 us
    dot_general x11, matrix products, mult(): return jnp.matmul(a, b, precision=high)  23.7 us
    ppermute x8, waiting for transfers between devices, extended(): lax.ppermute(head, axis, [((i + 1) % count, i) for i in range(ends)])  20.9 us
    ppermute x8, starting transfers between devices, extended(): lax.ppermute(head, axis, [((i + 1) % count, i) for i in range(ends)])  10.5 us
    slice x2, local copies, waits for them, and re-layouts, face_traces(): cube[..., :, :, last]  10 us
    unnamed x1, blocking collectives  8.88 us
    all_gather x1, blocking collectives, shards(): lax.all_gather(local_rhs, 'gx', axis=1, tiled=True)  7.16 us
  transfers between devices with their start and end apart: 16, of which 9 were waited for; matrix products, arithmetic and copies ran while one was open for 7% of the time, Pallas kernels for 0%

commit v1 on v0

v1 whole, which is shorter than its diff:
```python
import functools

import jax
import jax.numpy as jnp
from jax import lax
from jax.experimental import pallas as pl
from jax.experimental.pallas import tpu as pltpu
from jax.sharding import PartitionSpec as P

EDGE = 8
DOFS = 512
FACE = 64
COARSE = 8
CLUSTERS = 64
LANES = 128
META = 8

F32 = jnp.float32
BF16 = jnp.bfloat16
NT = (((1,), (1,)), ((), ()))
TN = (((0,), (0,)), ((), ()))


def selection():
    column = lane((1, 4 * FACE))
    face, a, b = column // FACE, column % FACE // EDGE, column % EDGE
    node = jnp.where(face < 2, a * 64 + face * 56 + b, a * 64 + b * 8 + (face - 2) * 7)
    at = lax.broadcasted_iota(jnp.int32, (DOFS, 4 * FACE), 0)
    return jnp.where(at == node, 1.0, 0.0).astype(BF16)


def halves(x):
    high = x.astype(BF16)
    return high, (x - high.astype(F32)).astype(BF16)


def dot(a, b, dims=(((1,), (0,)), ((), ()))):
    return lax.dot_general(a, b, dims, preferred_element_type=F32)


def dot3(a, b, dims=(((1,), (0,)), ((), ()))):
    return dot(a[0], b[0], dims) + (dot(a[0], b[1], dims) + dot(a[1], b[0], dims))


def dot3_few(a, b):
    n = a[0].shape[0]
    both = dot(jnp.concatenate(a, 0), b[0], NT)
    return both[:n] + (both[n:] + dot(a[0], b[1], NT))


def lane(shape):
    return lax.broadcasted_iota(jnp.int32, shape, len(shape) - 1)


def swap(x):
    return pltpu.roll(x, FACE, 1)


def pack0(t):
    n = t.shape[0] // 2
    return jnp.where(lane((n, LANES)) < FACE, t[:n], swap(t[n:]))


def pack7(t):
    n = t.shape[0] // 2
    return jnp.where(lane((n, LANES)) < FACE, swap(t[:n]), t[n:])


def unpack0(p):
    return jnp.concatenate([p, swap(p)], 0)


def unpack7(p):
    return jnp.concatenate([swap(p), p], 0)


def cell_rows(ref):
    ex, ey, ez = ref.shape
    rows = []
    for x in range(ex):
        rows.append(jnp.concatenate([ref[x, y : y + 1, :] for y in range(ey)], 1))
    return jnp.concatenate(rows, 0).astype(F32)


def reciprocal(rows):
    n = rows.shape[0]
    columns = (1.0 / jnp.concatenate([rows, jnp.ones((LANES - n, LANES), F32)], 0)).T
    return jnp.concatenate([jnp.broadcast_to(columns[:, x : x + 1], (LANES, LANES)) for x in range(n)], 0)


def as_row(rows):
    return jnp.concatenate([rows[x : x + 1] for x in range(rows.shape[0])], 1)


def onehot_rows(row):
    n = row.shape[1]
    at = lax.broadcasted_iota(jnp.int32, (CLUSTERS, n), 0).astype(F32)
    return jnp.where(at == row, 1.0, 0.0).astype(BF16)


def position(sizes):
    return lax.axis_index("gx"), lax.axis_index("gy"), lax.axis_index("gz")


def near_identity(s_ref, part):
    n = part.stop - part.start
    row = lax.broadcasted_iota(jnp.int32, (n, DOFS), 0) + part.start
    return halves(jnp.where(row == lane((n, DOFS)), 1.0, 0.0) - s_ref[part])


def start_all(pairs, sems, second=()):
    copies = [pltpu.make_async_copy(src, dst, sems.at[i]) for i, (src, dst) in enumerate(pairs)]
    for i, copy in enumerate(copies):
        copy.start(priority=1 if i in second else 0)
    return copies


def fetch(names, sems, rhs=None, s=None, m=None, l=None, rt=None, c=None):
    pairs = {"rhs": [rhs], "s": [s], "rt": [rt], "c": [c], "m": [], "l": []}
    for i in range(DOFS // LANES if m else 0):
        block = slice(i * LANES, (i + 1) * LANES)
        pairs["m"].append((m[0].at[block, block], m[1].at[i]))
    for f in range(6 if l else 0):
        g = f ^ 1
        pairs["l"].append((l[0].at[f * FACE : (f + 1) * FACE], l[1].at[g * FACE : (g + 1) * FACE]))
    counts = [len(pairs[name]) for name in names]
    first = [sum(counts[:i]) for i in range(len(names))]
    second = first[names.index("rhs")] if "rhs" in names else -1
    copies = start_all([pair for name in names for pair in pairs[name]], sems, [second])

    def wait(name):
        i = names.index(name)
        for copy in copies[first[i] : first[i] + counts[i]]:
            copy.wait()

    return wait


def diagonal_rows(d_ref):
    here = lax.broadcasted_iota(jnp.int32, (LANES, LANES), 0) == lane((LANES, LANES))
    return jnp.concatenate(
        [jnp.sum(jnp.where(here, d_ref[i], 0.0), 0, keepdims=True) for i in range(d_ref.shape[0])], 0
    )


def traces(u, split, pick, scale):
    lower = lane((u.shape[0], LANES)) < FACE
    picked = dot(split[0], pick) + dot(split[1], pick)
    x_pair = jnp.where(lower, u[:, :LANES], u[:, DOFS - LANES :]) * scale
    return x_pair, picked[:, :LANES] * scale, picked[:, LANES:] * scale


def smooth_kernel(sizes, rhs_hbm, s_hbm, coef_hbm, lab_hbm, rt_hbm, c_hbm,
                  uh_ref, ul_ref, th_ref, nh_ref, tr_ref, meta_ref, xy_ref, zu_ref, zd_ref, rt_ref, c_ref, rn_ref,
                  rhs_ref, s_ref, coef_ref, lab_ref, sems, late_sems):
    ngx, ngy, ngz = sizes
    gx, gy, gz = position(sizes)
    half = DOFS // 2
    blocks = [slice(0, half), slice(half, DOFS)]
    small = start_all([(coef_hbm, coef_ref), (lab_hbm, lab_ref)], sems)
    wait = fetch(
        ("rt", "c", "s"), late_sems, s=(s_hbm, s_ref), rt=(rt_hbm, rt_ref), c=(c_hbm, c_ref)
    )
    copies = [
        pltpu.make_async_copy(rhs_hbm.at[rows], rhs_ref.at[rows], sems.at[2 + i]) for i, rows in enumerate(blocks)
    ]
    for copy in copies:
        copy.start()
    ex, ey, ez = lab_ref.shape
    plane = ey * ez
    pick = selection()
    small[0].wait()
    small[1].wait()
    lab = cell_rows(lab_ref)
    counts = dot(jnp.ones((8, DOFS), BF16), onehot_rows(as_row(lab)), NT)
    weights = jnp.concatenate([1.0 + counts[0:1], jnp.ones((1, FACE), F32)], 1)
    meta = jnp.concatenate([lab, weights, jnp.zeros((META - 5, LANES), F32)], 0)
    meta_ref[:META] = meta
    meta_ref[META : META + ex] = cell_rows(coef_ref)
    rc = reciprocal(meta_ref[META : META + ex])

    wait("rt")
    wait("c")
    wait("s")
    near = near_identity(s_ref, slice(0, DOFS))
    nh_ref[...] = near[0]
    rn_ref[...] = dot3_few(halves(rt_ref[...]), near)
    pairs = []
    for rows, copy in zip(blocks, copies):
        copy.wait()
        rhs = rhs_ref[rows]
        t = dot3(halves(rhs), near)
        th_ref[rows] = t.astype(BF16)
        u = rhs - t
        split = halves(u)
        uh_ref[rows], ul_ref[rows] = split
        pairs.append(traces(u, split, pick, rc[rows]))
        for i, pair in enumerate(pairs[-1]):
            tr_ref[rows, i * LANES : (i + 1) * LANES] = pair
    x_pair, y_pair, z_pair = [jnp.concatenate([block[i] for block in pairs], 0) for i in range(3)]

    def y_rows(y):
        return jnp.concatenate(
            [y_pair[x * plane + y * ez : x * plane + (y + 1) * ez] for x in range(ex)], 0
        )

    def z_rows(z):
        return jnp.concatenate([z_pair[i * ez + z : i * ez + z + 1] for i in range(ex * ey)], 0)

    def send(ref, slot, payload):
        n = payload.shape[0]
        ref[slot, :n] = payload
        ref[slot, n:] = meta

    here = gx * ngy + gy
    send(xy_ref, jnp.where(gx < ngx - 1, here + ngy, here), pack7(x_pair[(ex - 1) * plane :]))
    send(xy_ref, jnp.where(gx > 0, here - ngy, here), pack0(x_pair[:plane]))
    send(xy_ref, jnp.where(gy < ngy - 1, here + 1, here), pack7(y_rows(ey - 1)))
    send(xy_ref, jnp.where(gy > 0, here - 1, here), pack0(y_rows(0)))
    zu_ref[...] = jnp.concatenate([pack7(z_rows(ez - 1)), meta], 0)
    zd_ref[...] = jnp.concatenate([pack0(z_rows(0)), meta], 0)


def receive(sizes, dims, xy_ref, zu_ref, zd_ref):
    ngx, ngy, ngz = sizes
    gx, gy, gz = position(sizes)

    def one(got, there):
        n = got.shape[0] - META
        payload = jnp.where(there, got[:n], 0.0)
        labels = jnp.where(there, got[n : n + dims[0]], -1.0)
        weights = jnp.where(there, got[n + dims[0] : n + dims[0] + 1], 1.0)
        return payload, labels, weights

    return [
        one(xy_ref[jnp.minimum(gx + 1, ngx - 1) * ngy + gy], gx < ngx - 1),
        one(xy_ref[jnp.maximum(gx - 1, 0) * ngy + gy], gx > 0),
        one(xy_ref[gx * ngy + jnp.minimum(gy + 1, ngy - 1)], gy < ngy - 1),
        one(xy_ref[gx * ngy + jnp.maximum(gy - 1, 0)], gy > 0),
        one(zd_ref[...], gz < ngz - 1),
        one(zu_ref[...], gz > 0),
    ]


def faces(f_ref, dims, tr_ref, around):
    ex, ey, ez = dims
    lower = lane((ez, LANES)) < FACE
    inner = lax.broadcasted_iota(jnp.int32, (ez, LANES), 0)
    none = jnp.zeros((ez, LANES), F32)
    outer = None
    if around is not None:
        outer = [(unpack0 if i % 2 == 0 else unpack7)(a[0]) for i, a in enumerate(around)]

    def local(i, pair):
        if tr_ref is None:
            return none
        return tr_ref[i * ez : (i + 1) * ez, pair]

    def remote(side, strip):
        return none if outer is None else outer[side][strip]

    for x in range(ex):
        for y in range(ey):
            i = x * ey + y
            rows = slice(i * ez, (i + 1) * ez)
            pair = slice(0, LANES)
            strip = slice(y * ez, (y + 1) * ez)
            above = local(i + ey, pair) if x < ex - 1 else remote(0, strip)
            below = local(i - ey, pair) if x > 0 else remote(1, strip)
            f_ref[rows, pair] = jnp.where(lower, above, below)
            pair = slice(LANES, 2 * LANES)
            strip = slice(x * ez, (x + 1) * ez)
            above = local(i + 1, pair) if y < ey - 1 else remote(2, strip)
            below = local(i - 1, pair) if y > 0 else remote(3, strip)
            f_ref[rows, pair] = jnp.where(lower, above, below)
            pair = slice(2 * LANES, 3 * LANES)
            above = below = none
            if tr_ref is not None:
                column = tr_ref[rows, pair]
                above = jnp.where(inner == ez - 1, 0.0, pltpu.roll(column, ez - 1, 0))
                below = jnp.where(inner == 0, 0.0, pltpu.roll(column, 1, 0))
            if outer is not None:
                above = jnp.where(inner == ez - 1, outer[4][i : i + 1], above)
                below = jnp.where(inner == 0, outer[5][i : i + 1], below)
            f_ref[rows, pair] = jnp.where(lower, above, below)


def prepare_kernel(dims, l_hbm, m_hbm, uh_ref, ul_ref, th_ref, nh_ref, tr_ref, rt_ref, rn_ref,
                   p_ref, own_ref, qh_ref, ql_ref, d_out_ref, l_ref, d_ref, f_ref, sems):
    wait = fetch(("l", "m"), sems, l=(l_hbm, l_ref), m=(m_hbm, d_ref))
    faces(f_ref, dims, tr_ref, None)
    inside = halves(f_ref[...])
    near = nh_ref[...]
    pick = selection()
    wait("l")
    wait("m")
    diagonal = diagonal_rows(d_ref)
    d_out_ref[...] = diagonal
    d = as_row(diagonal)
    lift = halves(l_ref[...])
    lrt = dot3_few(halves(rt_ref[...]), lift)
    zeros = jnp.zeros((COARSE, DOFS - FACE), F32)
    x0 = jnp.concatenate([lrt[:, :FACE], zeros], 1)
    x7 = jnp.concatenate([zeros, lrt[:, FACE:LANES]], 1)
    yz = lrt[:, LANES:]
    group = lane((COARSE, 4 * FACE)) // FACE
    spread = jnp.concatenate([jnp.where(group == f, yz, 0.0) for f in range(4)], 0)
    both = dot(jnp.concatenate(halves(spread), 0), pick, NT)
    yz = both[: 4 * COARSE] + both[4 * COARSE :]
    mrt = rt_ref[...] * d + rn_ref[...]
    q = jnp.concatenate([x0, x7, yz, mrt, jnp.zeros_like(mrt)], 0)
    rows = q.shape[0]
    both = dot(jnp.concatenate(halves(q), 0), near, NT)
    swept = q - (both[:rows] + both[rows:])
    split = halves(swept)
    of_t = dot(split[0], near, NT)
    of_f = halves(dot3_few(split, lift))
    qh_ref[...], ql_ref[...] = of_f
    of_u = halves(jnp.concatenate([q + swept * (1.0 - d), rt_ref[...]], 0))
    of_t = jnp.concatenate([of_t, rt_ref[...]], 0).astype(BF16)
    both = dot3_few(of_u, (uh_ref[...], ul_ref[...])) + dot(of_t, th_ref[...], NT)
    p_ref[...] = both[:rows] + dot3_few(of_f, inside)
    own_ref[...] = both[rows:]


def relax_kernel(sizes, dims, p_ref, own_ref, qh_ref, ql_ref, c_ref, meta_ref, xy_ref, zd_ref, zu_ref,
                 slots_ref, f_ref, bins_ref):
    ngx, ngy, ngz = sizes
    gx, gy, gz = position(sizes)
    ex, ey, ez = dims
    plane = ey * ez
    around = receive(sizes, dims, xy_ref, zu_ref, zd_ref)
    x_up, x_down, y_up, y_down, z_up, z_down = around
    q = qh_ref[...], ql_ref[...]
    rows = q[0].shape[0]
    keep = lane((rows, LANES)) < FACE

    def through(side, payload):
        pair = slice(side // 2 * LANES, (side // 2 + 1) * LANES)
        mine = keep if side % 2 == 0 else ~keep
        few = [jnp.where(mine, a[:, pair].astype(F32), 0.0).astype(BF16) for a in q]
        return dot3_few(few, halves(payload))

    added = []
    x_above, x_below = through(0, unpack0(x_up[0])), through(1, unpack7(x_down[0]))
    y_above, y_below = through(2, unpack0(y_up[0])), through(3, unpack7(y_down[0]))
    z_above, z_below = unpack0(z_up[0]), unpack7(z_down[0])
    inner = lax.broadcasted_iota(jnp.int32, (ez, LANES), 0)
    for i in range(ex * ey):
        f_ref[i * ez : (i + 1) * ez] = jnp.where(
            lane((ez, LANES)) < FACE,
            jnp.where(inner == ez - 1, z_above[i : i + 1], 0.0),
            jnp.where(inner == 0, z_below[i : i + 1], 0.0),
        )
    z_both = dot3_few([a[:, 2 * LANES :] for a in q], halves(f_ref[...]))
    at = lane((rows, LANES))
    for x in range(ex):
        tile = z_both[:, x * LANES : (x + 1) * LANES]
        up, down = (plane - ez - x * ez) % LANES, (LANES - x * ez) % LANES
        tile = tile + jnp.where(at >= plane - ez, pltpu.roll(y_above, up, 1) if up else y_above, 0.0)
        tile = tile + jnp.where(at < ez, pltpu.roll(y_below, down, 1) if down else y_below, 0.0)
        tile = tile + (x_above if x == ex - 1 else 0.0) + (x_below if x == 0 else 0.0)
        added.append(tile)
    p = p_ref[...] + jnp.concatenate(added, 1)
    own = own_ref[...]
    small = own - p[6 * COARSE : 7 * COARSE]
    p = p / as_row(meta_ref[META : META + ex])
    p_x0, p_x7, p_y0, p_y7, p_z0, p_z7 = [p[8 * f : 8 * f + 8] for f in range(6)]
    at = lane((COARSE, LANES))

    def tiles(a):
        return [a[:, x * LANES : (x + 1) * LANES] for x in range(ex)]

    none = jnp.zeros((COARSE, LANES), F32)
    total = []
    parts = [tiles(a) for a in (small, p_x0, p_x7, p_y0, p_y7, p_z0, p_z7)]
    for x in range(ex):
        s, _, _, y0, y7, z0, z7 = [a[x] for a in parts]
        s = s + (parts[1][x + 1] if x < ex - 1 else none)
        s = s + (parts[2][x - 1] if x > 0 else none)
        s = s + jnp.where(at < plane - ez, pltpu.roll(y0, LANES - ez, 1), 0.0)
        s = s + jnp.where(at >= ez, pltpu.roll(y7, ez, 1), 0.0)
        s = s + jnp.where(at % ez < ez - 1, pltpu.roll(z0, LANES - 1, 1), 0.0)
        s = s + jnp.where(at % ez > 0, pltpu.roll(z7, 1, 1), 0.0)
        total.append(s)
    total = jnp.concatenate(total, 1)

    def scatter(values, onehot):
        high, low = halves(values)
        out = dot(jnp.concatenate([high, low], 0), onehot, NT)
        return out[:COARSE] + out[COARSE:]

    def shifted(labels, shift, keep):
        return as_row(jnp.where(keep, pltpu.roll(labels, shift, 1), -1.0))

    rows = lane((ex, LANES))
    labels = meta_ref[0:ex]
    blocks = [
        (scatter(total, onehot_rows(as_row(labels))), meta_ref[ex : ex + 1]),
        (scatter(parts[2][ex - 1], onehot_rows(x_up[1][0:1])), x_up[2]),
        (scatter(parts[1][0], onehot_rows(x_down[1][ex - 1 : ex])), x_down[2]),
        (scatter(p_y7, onehot_rows(shifted(y_up[1], plane - ez, rows >= plane - ez))), y_up[2]),
        (scatter(p_y0, onehot_rows(shifted(y_down[1], ez, rows < ez))), y_down[2]),
        (scatter(p_z7, onehot_rows(shifted(z_up[1], ez - 1, rows % ez == ez - 1))), z_up[2]),
        (scatter(p_z0, onehot_rows(shifted(z_down[1], LANES - ez + 1, rows % ez == 0))), z_down[2]),
    ]
    raw = jnp.concatenate([z for z, _ in blocks], 1)
    mixed = raw + raw
    for k in range(COARSE):
        mixed = mixed - c_ref[:, k : k + 1] * raw[k : k + 1]

    def packed(block):
        rows = COARSE // 2
        return jnp.concatenate([block[:rows], block[rows:]], 1)

    b0, xu, xd, yu, yd, zu, zd = [packed(z / w[:, :FACE]) for z, w in blocks]
    a0, axu, axd, ayu, ayd, azu, azd = [
        packed(mixed[:, i * FACE : (i + 1) * FACE]) for i in range(len(blocks))
    ]

    count = slots_ref.shape[0]
    bins_ref[...] = jnp.zeros_like(bins_ref)

    def put(dx, dy, dz, share):
        there = (dy >= 0) & (dy < ngy) & (dz >= 0) & (dz < ngz)
        bins_ref[jnp.where(there, (dx * ngy + dy) * ngz + dz, count)] = share

    line = b0 + xu + xd
    sides = yu + yd + zu + zd
    for dx in range(ngx):
        same = (gx == dx).astype(F32)
        up = (gx + 1 == dx).astype(F32)
        down = (gx - 1 == dx).astype(F32)
        column = same * b0 + up * xu + down * xd
        put(dx, gy, gz, line + same * (sides + a0) + up * axu + down * axd)
        put(dx, gy + 1, gz, yu + column + same * ayu)
        put(dx, gy - 1, gz, yd + column + same * ayd)
        put(dx, gy, gz + 1, zu + column + same * azu)
        put(dx, gy, gz - 1, zd + column + same * azd)
    put(gx, gy + 2, gz, yu)
    put(gx, gy - 2, gz, yd)
    put(gx, gy, gz + 2, zu)
    put(gx, gy, gz - 2, zd)
    put(gx, gy + 1, gz + 1, yu + zu)
    put(gx, gy + 1, gz - 1, yu + zd)
    put(gx, gy - 1, gz + 1, yd + zu)
    put(gx, gy - 1, gz - 1, yd + zd)
    slots_ref[...] = bins_ref[:count]


def second_kernel(sizes, dims, rhs_hbm, s_hbm, l_hbm, uh_ref, ul_ref, tr_ref, d_ref, meta_ref, rt_ref, xy_ref, zd_ref, zu_ref,
                  second_ref, rs_ref, oh_ref, rhs_ref, s_ref, l_ref, f_ref, sems):
    wait = fetch(("l", "s", "rhs"), sems, rhs=(rhs_hbm, rhs_ref), s=(s_hbm, s_ref), l=(l_hbm, l_ref))
    ex = dims[0]
    faces(f_ref, dims, tr_ref, receive(sizes, dims, xy_ref, zu_ref, zd_ref))
    onehot = onehot_rows(as_row(meta_ref[:ex]))
    oh_ref[...] = jnp.concatenate([onehot, onehot], 0).astype(F32).T.astype(BF16)
    rt = halves(rt_ref[...])
    rs_ref[...] = jnp.concatenate([rt[0], rt[0], rt[1], jnp.zeros_like(rt[0])], 0)
    wait("l")
    r1 = dot3(halves(f_ref[...]), halves(l_ref[...]))
    wait("s")
    near = near_identity(s_ref, slice(0, DOFS))
    wait("rhs")
    u = uh_ref[...].astype(F32) + ul_ref[...].astype(F32)
    d = as_row(d_ref[...])
    r1 = r1 + dot3(halves(rhs_ref[...] - u), near) + u * (1.0 - d)
    v = u + (r1 - dot3(halves(r1), near))
    rc = reciprocal(meta_ref[META : META + ex])
    second_ref[...] = v * jnp.concatenate([rc] * (DOFS // LANES), 1)


def correct_kernel(second_ref, slots_ref, meta_ref, oh_ref, rs_ref, out_hbm, out_ref, sems):
    total = jnp.sum(slots_ref[...], 0)
    ztwo = jnp.concatenate([total[:, :FACE], total[:, FACE:]], 0) / meta_ref[4:5, :FACE]
    high, low = halves(ztwo)
    stacked = jnp.concatenate([high, low, high, jnp.zeros_like(high)], 0)
    prolonged = dot(stacked, rs_ref[...], TN)
    prolonged = jnp.concatenate(halves(prolonged), 0)
    chunk = DOFS // sems.shape[0]
    copies = []
    for i in range(sems.shape[0]):
        rows = slice(i * chunk, (i + 1) * chunk)
        out_ref[rows] = second_ref[rows] + dot(oh_ref[rows], prolonged)
        copy = pltpu.make_async_copy(out_ref.at[rows], out_hbm.at[rows], sems.at[i])
        copy.start()
        copies.append(copy)
    for copy in copies:
        copy.wait()


def shards(sizes, rhs, coef, mass, smoother, lift, restrict, coarse_block_matrix, element_cluster_index):
    ngx, ngy, ngz = sizes
    dims = coef.shape
    ex, ey, ez = dims
    flat = rhs.reshape(ex * ey * ez, DOFS)
    face = ey * ez * FACE // LANES
    tip = ex * ey * FACE // LANES
    params = pltpu.CompilerParams(vmem_limit_bytes=40 * 1024 * 1024)
    shape = jax.ShapeDtypeStruct
    hbm = pl.BlockSpec(memory_space=pltpu.HBM)
    vmem = pl.BlockSpec(memory_space=pltpu.VMEM)
    cost = pl.CostEstimate(flops=2 * 10**9, bytes_accessed=4 * 2**20, transcendentals=0)
    def far(*arrays):
        return [pltpu.with_memory_space_constraint(a, pltpu.HBM) for a in arrays]

    full = shape((DOFS, DOFS), F32)
    split = shape((DOFS, DOFS), BF16)
    count = ngx * ngy * ngz
    wide = shape((8 * COARSE, 3 * LANES), BF16)
    few = shape((COARSE, DOFS), F32)
    uh, ul, th, nh, tr, meta, xy, zu, zd, rt, c, rn = pl.pallas_call(
        functools.partial(smooth_kernel, sizes),
        out_shape=(
            split,
            split,
            split,
            split,
            shape((DOFS, 3 * LANES), F32),
            shape((2 * META, LANES), F32),
            shape((ngx * ngy, face + META, LANES), F32),
            shape((tip + META, LANES), F32),
            shape((tip + META, LANES), F32),
            few,
            shape((COARSE, COARSE), F32),
            few,
        ),
        in_specs=[hbm] * 6,
        scratch_shapes=[
            pltpu.VMEM((DOFS, DOFS), F32),
            pltpu.VMEM((DOFS, DOFS), F32),
            pltpu.VMEM(dims, F32),
            pltpu.VMEM(dims, jnp.int32),
            pltpu.SemaphoreType.DMA((4,)),
            pltpu.SemaphoreType.DMA((3,)),
        ],
        compiler_params=params,
        cost_estimate=cost,
        name="smooth",
    )(*far(flat, smoother, coef, element_cluster_index, restrict.T, coarse_block_matrix))
    zd = lax.ppermute(zd, "gz", [(i + 1, i) for i in range(ngz - 1)])
    zu = lax.ppermute(zu, "gz", [(i, i + 1) for i in range(ngz - 1)])
    xy = lax.all_to_all(xy, ("gx", "gy"), 0, 0, tiled=True)
    p, own, fh, fl, d = pl.pallas_call(
        functools.partial(prepare_kernel, dims),
        out_shape=(shape((8 * COARSE, DOFS), F32), few, wide, wide, shape((DOFS // LANES, LANES), F32)),
        in_specs=[hbm] * 2 + [vmem] * 7,
        scratch_shapes=[
            pltpu.VMEM((3 * LANES, DOFS), F32),
            pltpu.VMEM((DOFS // LANES, LANES, LANES), F32),
            pltpu.VMEM((DOFS, 3 * LANES), F32),
            pltpu.SemaphoreType.DMA((10,)),
        ],
        compiler_params=params,
        cost_estimate=cost,
        name="prepare",
    )(*far(lift, mass), uh, ul, th, nh, tr, rt, rn)
    slots = pl.pallas_call(
        functools.partial(relax_kernel, sizes, dims),
        out_shape=shape((count, COARSE // 2, LANES), F32),
        scratch_shapes=[
            pltpu.VMEM((DOFS, LANES), F32),
            pltpu.VMEM((count + 1, COARSE // 2, LANES), F32),
        ],
        compiler_params=params,
        cost_estimate=cost,
        name="relax",
    )(p, own, fh, fl, c, meta, xy, zd, zu)
    slots = lax.all_to_all(slots, ("gx", "gy", "gz"), 0, 0, tiled=True)
    second, rs, oh = pl.pallas_call(
        functools.partial(second_kernel, sizes, dims),
        out_shape=(
            full,
            shape((4 * COARSE, DOFS), BF16),
            shape((DOFS, LANES), BF16),
        ),
        in_specs=[hbm] * 3 + [vmem] * 9,
        scratch_shapes=[
            pltpu.VMEM((DOFS, DOFS), F32),
            pltpu.VMEM((DOFS, DOFS), F32),
            pltpu.VMEM((3 * LANES, DOFS), F32),
            pltpu.VMEM((DOFS, 3 * LANES), F32),
            pltpu.SemaphoreType.DMA((8,)),
        ],
        compiler_params=params,
        cost_estimate=cost,
        name="second",
    )(*far(flat, smoother, lift), uh, ul, tr, d, meta, rt, xy, zd, zu)
    out = pl.pallas_call(
        correct_kernel,
        out_shape=shape((DOFS, DOFS), F32),
        out_specs=hbm,
        scratch_shapes=[pltpu.VMEM((DOFS, DOFS), F32), pltpu.SemaphoreType.DMA((4,))],
        compiler_params=params,
        name="correct",
    )(second, slots, meta, oh, rs)
    return out.reshape(rhs.shape)


def solution(mesh):
    sizes = (mesh.shape["gx"], mesh.shape["gy"], mesh.shape["gz"])
    cells = P("gx", "gy", "gz")
    return jax.shard_map(
        functools.partial(shards, sizes),
        mesh=mesh,
        in_specs=(P("gx", "gy", "gz", None), cells, P(), P(), P(), P(), P(), cells),
        out_specs=P("gx", "gy", "gz", None),
        check_vma=False,
    )
```

time: 160 us -> 35.2 us (0.22)
  local copies, waits for them, and re-layouts: 52.7 us -> 0 us
  matrix products: 23.7 us -> 0 us
  starting transfers between devices: 38.1 us -> 16.3 us
  waiting for transfers between devices: 22.7 us -> 2.91 us
  blocking collectives: 16 us -> 0 us
  Pallas kernels: 0 us -> 15.6 us
  other arithmetic: 4.87 us -> 0 us
    ppermute x16 -> x2, starting transfers between devices: 38.1 us -> 5.83 us  [the longest x1 4.55 us: shards(): zu = lax.ppermute(zu, 'gz', [(i, i + 1) for i in range(ngz - 1)])]
    another operation x16 -> x0, local copies, waits for them, and re-layouts: 27.6 us -> none  [face_traces(): return jnp.concatenate([p.reshape(lead + (FACE,)) for p in parts], -1)]
    dot_general x11 -> x0, matrix products: 23.7 us -> none  [mult(): return jnp.matmul(a, b, precision=high)]
    ppermute x16 -> x2, waiting for transfers between devices: 22.7 us -> 0.01 us  [the longest x1 0.01 us: shards(): zd = lax.ppermute(zd, 'gz', [(i + 1, i) for i in range(ngz - 1)])]
    pallas_call x0 -> x5, Pallas kernels: none -> 15.6 us  [the longest x1 4.97 us: shards(): pl.pallas_call(functools.partial(smooth_kernel, sizes), out_shape=(split,...]
    slice x4 -> x0, local copies, waits for them, and re-layouts: 10.8 us -> none  [the longest x2 10 us: face_traces(): cube[..., :, :, last]]
    all_to_all x0 -> x2, starting transfers between devices: none -> 10.5 us  [the longest x1 5.32 us: shards(): slots = lax.all_to_all(slots, ('gx', 'gy', 'gz'), 0, 0, tiled=True)]
    unnamed x1 -> x0, blocking collectives: 8.88 us -> none
  transfers between devices with their start and end apart: 16 -> 4, of which waited for: 9 -> 1; matrix products, arithmetic and copies ran while one was open for 7% -> 0% of each run, Pallas kernels for 0% -> 22%
where the time goes in v1:
time: 35.2 us; the launch traced here: 34.9 us
  starting transfers between devices  16.3 us (46%)
  Pallas kernels  15.6 us (44%)
  waiting for transfers between devices  2.91 us (8%)
    all_to_all x1, starting transfers between devices, shards(): slots = lax.all_to_all(slots, ('gx', 'gy', 'gz'), 0, 0, tiled=True)  5.32 us
    all_to_all x1, starting transfers between devices, shards(): xy = lax.all_to_all(xy, ('gx', 'gy'), 0, 0, tiled=True)  5.18 us
    pallas_call x1, Pallas kernels, shards(): pl.pallas_call(functools.partial(smooth_kernel, sizes), out_shape=(split,...  4.97 us
    ppermute x1, starting transfers between devices, shards(): zu = lax.ppermute(zu, 'gz', [(i, i + 1) for i in range(ngz - 1)])  4.55 us
    pallas_call x1, Pallas kernels, shards(): pl.pallas_call(functools.partial(second_kernel, sizes, dims), out_shape=(...  4.37 us
    pallas_call x1, Pallas kernels, shards(): pl.pallas_call(functools.partial(prepare_kernel, dims), out_shape=(shape(...  3.24 us
    all_to_all x1, waiting for transfers between devices, shards(): slots = lax.all_to_all(slots, ('gx', 'gy', 'gz'), 0, 0, tiled=True)  2.9 us
    pallas_call x1, Pallas kernels, shards(): pl.pallas_call(functools.partial(relax_kernel, sizes, dims), out_shape=sh...  1.52 us
  transfers between devices with their start and end apart: 4, of which 1 were waited for; matrix products, arithmetic and copies ran while one was open for 0% of the time, Pallas kernels for 22%

profile of v1, /device:TPU:0, one launch (start us, length us, event | category | flops | bytes accessed | tf_op | source)
XLA Modules:
  0.0 34.9 jit_solution(18174914529677133980)
XLA Ops:
  0.0 5.0 %smooth.1 = (bf16[512,512]{1,0:T(8,128)(2,1)S(1)}, bf16[512,512]{1,0:T(8,128)(2,1)S(1)}, bf16[512,512]{1,0:T(8,128)(2,1)S(1)}, bf16[512,512]{1,0:T(8,128)(2,1)S(...) custom-call(f32[512,512]{1,0:T(8,128)} %bitcast.3, ...), custom_call_target="tpu_custom_call" | custom-call | flops 2000000000 | bytes 4194304 | tf_op jit(solution)/shard_map/smooth/pallas_call | solution.py:512
  5.0 5.2 %all-to-all-start = ((f32[8,72,128]{2,1,0:T(8,128)}), f32[8,72,128]{2,1,0:T(8,128)S(1)}, u32[]{:S(2)}, u32[]{:S(2)}) async-start(f32[8,72,128]{2,1,0:T(8,128)} %get-tuple-element.34), calls=%async_computation | async-start | bytes 589824 | tf_op jit(solution)/shard_map/all_to_all | solution.py:543
  10.2 1.3 %collective-permute-start = (f32[16,128]{1,0:T(8,128)S(1)}, f32[16,128]{1,0:T(8,128)S(1)}, u32[]{:S(2)}, u32[]{:S(2)}) collective-permute-start(f32[16,128]{1,0:T(8,128)S(1)} %get-tuple-element.35), channel_id=1, source_target_pairs={{1,0},{2,1},{3,2},{5,4},{6,5},{7,6},{9,8},{10,9},{11,10},{13,12},{... | collective-permute-start | bytes 24584 | tf_op jit(solution)/shard_map/ppermute | solution.py:541
  11.4 4.5 %collective-permute-start.1 = (f32[16,128]{1,0:T(8,128)S(1)}, f32[16,128]{1,0:T(8,128)S(1)}, u32[]{:S(2)}, u32[]{:S(2)}) collective-permute-start(f32[16,128]{1,0:T(8,128)S(1)} %get-tuple-element.36), channel_id=1, source_target_pairs={{0,1},{1,2},{2,3},{4,5},{5,6},{6,7},{8,9},{9,10},{10,11},{12,13},{... | collective-permute-start | bytes 24584 | tf_op jit(solution)/shard_map/ppermute | solution.py:542
  16.0 3.2 %prepare.1 = (f32[64,512]{1,0:T(8,128)S(1)}, f32[8,512]{1,0:T(8,128)S(1)}, bf16[64,384]{1,0:T(8,128)(2,1)S(1)}, bf16[64,384]{1,0:T(8,128)(2,1)S(1)}, f32[4,128]{1,0:T(4,128)S(1)}) custom-call(f32[384,512]{1,0:T(8,128)} %l_hbm.3, f32[512,512]{1,0:T(8,128)} %m_hbm.1, bf16[512,512]{1,0:T(8,128)(2,1)S(1)} %get-tuple-element.25.uh_ref, ...), custom_call_target="tpu_custom_call" | custom-call | flops 2000000000 | bytes 4194304 | tf_op jit(solution)/shard_map/prepare/pallas_call | solution.py:544
  19.2 0.0 collective-permute-done.zd_ref
  19.3 0.0 collective-permute-done.1.zu_ref
  19.3 0.0 all-to-all-done.xy_ref
  19.3 1.5 %relax.1 = f32[32,4,128]{2,1,0:T(4,128)} custom-call(f32[64,512]{1,0:T(8,128)S(1)} %get-tuple-element.38.p_ref, f32[8,512]{1,0:T(8,128)S(1)} %get-tuple-element.39.own_ref, bf16[64,384]{1,0:T(8,128)(2,1)S(1)} %get-tuple-element.40.qh_ref, bf16[64,384]{1,0:T(8,128)(2,1)S(1)} %get-tuple-element.41.ql_ref, f32[8,8]{1,0:T(8,128)S(1)} %get-tuple-element.42.c_ref, ...), custom_call_target="tpu_custom_call" | custom-call | flops 2000000000 | bytes 4194304 | tf_op jit(solution)/shard_map/relax/pallas_call | solution.py:558
  20.8 5.3 %all-to-all-start.1 = ((f32[32,4,128]{2,1,0:T(4,128)}), f32[32,4,128]{2,1,0:T(4,128)S(1)}, u32[]{:S(2)}, u32[]{:S(2)}) async-start(f32[32,4,128]{2,1,0:T(4,128)} %relax.1), calls=%async_computation.1 | async-start | bytes 131072 | tf_op jit(solution)/shard_map/all_to_all | solution.py:569
  26.1 4.4 %second.1 = (f32[512,512]{1,0:T(8,128)S(1)}, bf16[32,512]{1,0:T(8,128)(2,1)S(1)}, bf16[512,128]{1,0:T(8,128)(2,1)S(1)}) custom-call(f32[512,512]{1,0:T(8,128)} %bitcast.4, f32[512,512]{1,0:T(8,128)} %s_hbm.3, f32[384,512]{1,0:T(8,128)} %l_hbm.3, bf16[512,512]{1,0:T(8,128)(2,1)S(1)} %get-tuple-element.25.uh_ref, ...), custom_call_target="tpu_custom_call" | custom-call | flops 2000000000 | bytes 4194304 | tf_op jit(solution)/shard_map/second/pallas_call | solution.py:570
  30.5 2.9 %all-to-all-done.1.slots_ref = f32[32,4,128]{2,1,0:T(4,128)S(1)} async-done(((f32[32,4,128]{2,1,0:T(4,128)}), f32[32,4,128]{2,1,0:T(4,128)S(1)}, u32[]{:S(2)}, u32[]{:S(2)}) %all-to-all-start.1) | async-done | bytes 65568 | tf_op jit(solution)/shard_map/all_to_all | solution.py:569
  33.4 1.5 %correct.1 = f32[512,512]{1,0:T(8,128)} custom-call(f32[512,512]{1,0:T(8,128)S(1)} %get-tuple-element.37.second_ref, f32[32,4,128]{2,1,0:T(4,128)S(1)} %all-to-all-done.1.slots_ref, f32[16,128]{1,0:T(8,128)S(1)} %get-tuple-element.33.meta_ref, bf16[512,128]{1,0:T(8,128)(2,1)S(1)} %get-tuple-element.43.oh_ref, bf16[32,512]{1,0:T(8,128)(2,1)S(1)} %get-tuple-element.44.rs_ref), custom_call_target="tpu_custom_call" | custom-call | tf_op jit(solution)/shard_map/correct/pallas_call | solution.py:589
Async XLA Ops:
  5.0 14.3 %all-to-all-start = ((f32[8,72,128]{2,1,0:T(8,128)}), f32[8,72,128]{2,1,0:T(8,128)S(1)}, u32[]{:S(2)}, u32[]{:S(2)}) async-start(f32[8,72,128]{2,1,0:T(8,128)} %get-tuple-element.34), calls=%async_computation | async-start | bytes 589824 | tf_op jit(solution)/shard_map/all_to_all | solution.py:543
  10.2 9.1 %collective-permute-start = (f32[16,128]{1,0:T(8,128)S(1)}, f32[16,128]{1,0:T(8,128)S(1)}, u32[]{:S(2)}, u32[]{:S(2)}) collective-permute-start(f32[16,128]{1,0:T(8,128)S(1)} %get-tuple-element.35), channel_id=1, source_target_pairs={{1,0},{2,1},{3,2},{5,4},{6,5},{7,6},{9,8},{10,9},{11,10},{13,12},{... | collective-permute-start | bytes 24584 | tf_op jit(solution)/shard_map/ppermute | solution.py:541
  11.4 7.8 %collective-permute-start.1 = (f32[16,128]{1,0:T(8,128)S(1)}, f32[16,128]{1,0:T(8,128)S(1)}, u32[]{:S(2)}, u32[]{:S(2)}) collective-permute-start(f32[16,128]{1,0:T(8,128)S(1)} %get-tuple-element.36), channel_id=1, source_target_pairs={{0,1},{1,2},{2,3},{4,5},{5,6},{6,7},{8,9},{9,10},{10,11},{12,13},{... | collective-permute-start | bytes 24584 | tf_op jit(solution)/shard_map/ppermute | solution.py:542
  20.8 12.6 %all-to-all-start.1 = ((f32[32,4,128]{2,1,0:T(4,128)}), f32[32,4,128]{2,1,0:T(4,128)S(1)}, u32[]{:S(2)}, u32[]{:S(2)}) async-start(f32[32,4,128]{2,1,0:T(4,128)} %relax.1), calls=%async_computation.1 | async-start | bytes 131072 | tf_op jit(solution)/shard_map/all_to_all | solution.py:569

commit v2 on v1

--- a/solution.py
+++ b/solution.py
@@ -82,6 +82,10 @@
     return jnp.concatenate(rows, 0).astype(F32)
 
 
+def face_order(lift):
+    return jnp.concatenate([lift[(f ^ 1) * FACE : ((f ^ 1) + 1) * FACE] for f in range(6)], 0)
+
+
 def reciprocal(rows):
     n = rows.shape[0]
     columns = (1.0 / jnp.concatenate([rows, jnp.ones((LANES - n, LANES), F32)], 0)).T
@@ -115,14 +119,11 @@
     return copies
 
 
-def fetch(names, sems, rhs=None, s=None, m=None, l=None, rt=None, c=None):
-    pairs = {"rhs": [rhs], "s": [s], "rt": [rt], "c": [c], "m": [], "l": []}
+def fetch(names, sems, rhs=None, s=None, m=None, l=None):
+    pairs = {"rhs": [rhs], "s": [s], "l": [l], "m": []}
     for i in range(DOFS // LANES if m else 0):
         block = slice(i * LANES, (i + 1) * LANES)
         pairs["m"].append((m[0].at[block, block], m[1].at[i]))
-    for f in range(6 if l else 0):
-        g = f ^ 1
-        pairs["l"].append((l[0].at[f * FACE : (f + 1) * FACE], l[1].at[g * FACE : (g + 1) * FACE]))
     counts = [len(pairs[name]) for name in names]
     first = [sum(counts[:i]) for i in range(len(names))]
     second = first[names.index("rhs")] if "rhs" in names else -1
@@ -151,26 +152,27 @@
 
 
 def smooth_kernel(sizes, rhs_hbm, s_hbm, coef_hbm, lab_hbm, rt_hbm, c_hbm,
-                  uh_ref, ul_ref, th_ref, nh_ref, tr_ref, meta_ref, xy_ref, zu_ref, zd_ref, rt_ref, c_ref, rn_ref,
-                  rhs_ref, s_ref, coef_ref, lab_ref, sems, late_sems):
+                  uh_ref, ul_ref, th_ref, nh_ref, tr_ref, meta_ref, xy_ref, z1_ref, z2_ref, rt_ref, c_ref, rn_ref,
+                  rhs_ref, s_ref, coef_ref, lab_ref, t_ref, sems):
     ngx, ngy, ngz = sizes
     gx, gy, gz = position(sizes)
     half = DOFS // 2
     blocks = [slice(0, half), slice(half, DOFS)]
-    small = start_all([(coef_hbm, coef_ref), (lab_hbm, lab_ref)], sems)
-    wait = fetch(
-        ("rt", "c", "s"), late_sems, s=(s_hbm, s_ref), rt=(rt_hbm, rt_ref), c=(c_hbm, c_ref)
-    )
-    copies = [
-        pltpu.make_async_copy(rhs_hbm.at[rows], rhs_ref.at[rows], sems.at[2 + i]) for i, rows in enumerate(blocks)
-    ]
-    for copy in copies:
-        copy.start()
+    pairs = [(coef_hbm, coef_ref), (lab_hbm, lab_ref), (rt_hbm, rt_ref), (c_hbm, c_ref)]
+    for part in blocks:
+        quarters = [slice(part.start + i * half // 2, part.start + (i + 1) * half // 2) for i in range(2)]
+        pairs += [(s_hbm.at[rows], s_ref.at[rows]) for rows in quarters]
+        pairs += [(rhs_hbm.at[rows, part], rhs_ref.at[rows, part]) for rows in blocks]
+    copies = start_all(pairs, sems)
+
+    def wait(first, count):
+        for copy in copies[first : first + count]:
+            copy.wait()
+
     ex, ey, ez = lab_ref.shape
     plane = ey * ez
     pick = selection()
-    small[0].wait()
-    small[1].wait()
+    wait(0, 4)
     lab = cell_rows(lab_ref)
     counts = dot(jnp.ones((8, DOFS), BF16), onehot_rows(as_row(lab)), NT)
     weights = jnp.concatenate([1.0 + counts[0:1], jnp.ones((1, FACE), F32)], 1)
@@ -179,19 +181,26 @@
     meta_ref[META : META + ex] = cell_rows(coef_ref)
     rc = reciprocal(meta_ref[META : META + ex])
 
-    wait("rt")
-    wait("c")
-    wait("s")
-    near = near_identity(s_ref, slice(0, DOFS))
-    nh_ref[...] = near[0]
-    rn_ref[...] = dot3_few(halves(rt_ref[...]), near)
+    rt = halves(rt_ref[...])
+
+    def near_part(part):
+        near = near_identity(s_ref, part)
+        nh_ref[part] = near[0]
+        rn_ref[:, part] = dot3_few(rt, near)
+        return near
+
+    wait(4, 2)
+    near = near_part(blocks[0])
+    wait(6, 2)
+    t_ref[...] = dot3(halves(rhs_ref[:, blocks[0]]), near)
+    wait(8, 2)
+    near = near_part(blocks[1])
+    wait(10, 2)
     pairs = []
-    for rows, copy in zip(blocks, copies):
-        copy.wait()
-        rhs = rhs_ref[rows]
-        t = dot3(halves(rhs), near)
+    for rows in blocks:
+        t = t_ref[rows] + dot3(halves(rhs_ref[rows, blocks[1]]), near)
         th_ref[rows] = t.astype(BF16)
-        u = rhs - t
+        u = rhs_ref[rows] - t
         split = halves(u)
         uh_ref[rows], ul_ref[rows] = split
         pairs.append(traces(u, split, pick, rc[rows]))
@@ -217,13 +226,16 @@
     send(xy_ref, jnp.where(gx > 0, here - ngy, here), pack0(x_pair[:plane]))
     send(xy_ref, jnp.where(gy < ngy - 1, here + 1, here), pack7(y_rows(ey - 1)))
     send(xy_ref, jnp.where(gy > 0, here - 1, here), pack0(y_rows(0)))
-    zu_ref[...] = jnp.concatenate([pack7(z_rows(ez - 1)), meta], 0)
-    zd_ref[...] = jnp.concatenate([pack0(z_rows(0)), meta], 0)
-
-
-def receive(sizes, dims, xy_ref, zu_ref, zd_ref):
+    odd = lax.rem(gz, 2) == 1
+    up, down = pack7(z_rows(ez - 1)), pack0(z_rows(0))
+    z1_ref[...] = jnp.concatenate([jnp.where(odd, up, down), meta], 0)
+    z2_ref[...] = jnp.concatenate([jnp.where(odd, down, up), meta], 0)
+
+
+def receive(sizes, dims, xy_ref, z1_ref, z2_ref):
     ngx, ngy, ngz = sizes
     gx, gy, gz = position(sizes)
+    odd = lax.rem(gz, 2) == 1
 
     def one(got, there):
         n = got.shape[0] - META
@@ -237,8 +249,8 @@
         one(xy_ref[jnp.maximum(gx - 1, 0) * ngy + gy], gx > 0),
         one(xy_ref[gx * ngy + jnp.minimum(gy + 1, ngy - 1)], gy < ngy - 1),
         one(xy_ref[gx * ngy + jnp.maximum(gy - 1, 0)], gy > 0),
-        one(zd_ref[...], gz < ngz - 1),
-        one(zu_ref[...], gz > 0),
+        one(jnp.where(odd, z1_ref[...], z2_ref[...]), gz < ngz - 1),
+        one(jnp.where(odd, z2_ref[...], z1_ref[...]), gz > 0),
     ]
 
 
@@ -297,7 +309,7 @@
     diagonal = diagonal_rows(d_ref)
     d_out_ref[...] = diagonal
     d = as_row(diagonal)
-    lift = halves(l_ref[...])
+    lift = halves(face_order(l_ref[...]))
     lrt = dot3_few(halves(rt_ref[...]), lift)
     zeros = jnp.zeros((COARSE, DOFS - FACE), F32)
     x0 = jnp.concatenate([lrt[:, :FACE], zeros], 1)
@@ -316,20 +328,20 @@
     of_t = dot(split[0], near, NT)
     of_f = halves(dot3_few(split, lift))
     qh_ref[...], ql_ref[...] = of_f
-    of_u = halves(jnp.concatenate([q + swept * (1.0 - d), rt_ref[...]], 0))
-    of_t = jnp.concatenate([of_t, rt_ref[...]], 0).astype(BF16)
-    both = dot3_few(of_u, (uh_ref[...], ul_ref[...])) + dot(of_t, th_ref[...], NT)
-    p_ref[...] = both[:rows] + dot3_few(of_f, inside)
-    own_ref[...] = both[rows:]
-
-
-def relax_kernel(sizes, dims, p_ref, own_ref, qh_ref, ql_ref, c_ref, meta_ref, xy_ref, zd_ref, zu_ref,
+    of_u = halves(jnp.concatenate([q + swept * (1.0 - d), rt_ref[...] + rn_ref[...]], 0))
+    by_t = dot(jnp.concatenate([of_t, rn_ref[...]], 0).astype(BF16), th_ref[...], NT)
+    by_u = dot3_few(of_u, (uh_ref[...], ul_ref[...]))
+    p_ref[...] = by_u[:rows] + by_t[:rows] + dot3_few(of_f, inside)
+    own_ref[...] = by_u[rows:] + by_t[rows:]
+
+
+def relax_kernel(sizes, dims, p_ref, own_ref, qh_ref, ql_ref, c_ref, meta_ref, xy_ref, z1_ref, z2_ref,
                  slots_ref, f_ref, bins_ref):
     ngx, ngy, ngz = sizes
     gx, gy, gz = position(sizes)
     ex, ey, ez = dims
     plane = ey * ez
-    around = receive(sizes, dims, xy_ref, zu_ref, zd_ref)
+    around = receive(sizes, dims, xy_ref, z1_ref, z2_ref)
     x_up, x_down, y_up, y_down, z_up, z_down = around
     q = qh_ref[...], ql_ref[...]
     rows = q[0].shape[0]
@@ -448,17 +460,17 @@
     slots_ref[...] = bins_ref[:count]
 
 
-def second_kernel(sizes, dims, rhs_hbm, s_hbm, l_hbm, uh_ref, ul_ref, tr_ref, d_ref, meta_ref, rt_ref, xy_ref, zd_ref, zu_ref,
+def second_kernel(sizes, dims, rhs_hbm, s_hbm, l_hbm, uh_ref, ul_ref, tr_ref, d_ref, meta_ref, rt_ref, xy_ref, z1_ref, z2_ref,
                   second_ref, rs_ref, oh_ref, rhs_ref, s_ref, l_ref, f_ref, sems):
     wait = fetch(("l", "s", "rhs"), sems, rhs=(rhs_hbm, rhs_ref), s=(s_hbm, s_ref), l=(l_hbm, l_ref))
     ex = dims[0]
-    faces(f_ref, dims, tr_ref, receive(sizes, dims, xy_ref, zu_ref, zd_ref))
+    faces(f_ref, dims, tr_ref, receive(sizes, dims, xy_ref, z1_ref, z2_ref))
     onehot = onehot_rows(as_row(meta_ref[:ex]))
     oh_ref[...] = jnp.concatenate([onehot, onehot], 0).astype(F32).T.astype(BF16)
     rt = halves(rt_ref[...])
     rs_ref[...] = jnp.concatenate([rt[0], rt[0], rt[1], jnp.zeros_like(rt[0])], 0)
     wait("l")
-    r1 = dot3(halves(f_ref[...]), halves(l_ref[...]))
+    r1 = dot3(halves(f_ref[...]), halves(face_order(l_ref[...])))
     wait("s")
     near = near_identity(s_ref, slice(0, DOFS))
     wait("rhs")
@@ -509,7 +521,7 @@
     count = ngx * ngy * ngz
     wide = shape((8 * COARSE, 3 * LANES), BF16)
     few = shape((COARSE, DOFS), F32)
-    uh, ul, th, nh, tr, meta, xy, zu, zd, rt, c, rn = pl.pallas_call(
+    uh, ul, th, nh, tr, meta, xy, z1, z2, rt, c, rn = pl.pallas_call(
         functools.partial(smooth_kernel, sizes),
         out_shape=(
             split,
@@ -531,15 +543,19 @@
             pltpu.VMEM((DOFS, DOFS), F32),
             pltpu.VMEM(dims, F32),
             pltpu.VMEM(dims, jnp.int32),
-            pltpu.SemaphoreType.DMA((4,)),
-            pltpu.SemaphoreType.DMA((3,)),
+            pltpu.VMEM((DOFS, DOFS), F32),
+            pltpu.SemaphoreType.DMA((12,)),
         ],
         compiler_params=params,
         cost_estimate=cost,
         name="smooth",
     )(*far(flat, smoother, coef, element_cluster_index, restrict.T, coarse_block_matrix))
-    zd = lax.ppermute(zd, "gz", [(i + 1, i) for i in range(ngz - 1)])
-    zu = lax.ppermute(zu, "gz", [(i, i + 1) for i in range(ngz - 1)])
+    def swaps(start):
+        pairs = [(i, i + 1) for i in range(start, ngz - 1, 2)]
+        return pairs + [(j, i) for i, j in pairs]
+
+    z1 = lax.ppermute(z1, "gz", swaps(1))
+    z2 = lax.ppermute(z2, "gz", swaps(0))
     xy = lax.all_to_all(xy, ("gx", "gy"), 0, 0, tiled=True)
     p, own, fh, fl, d = pl.pallas_call(
         functools.partial(prepare_kernel, dims),
@@ -549,7 +565,7 @@
             pltpu.VMEM((3 * LANES, DOFS), F32),
             pltpu.VMEM((DOFS // LANES, LANES, LANES), F32),
             pltpu.VMEM((DOFS, 3 * LANES), F32),
-            pltpu.SemaphoreType.DMA((10,)),
+            pltpu.SemaphoreType.DMA((5,)),
         ],
         compiler_params=params,
         cost_estimate=cost,
@@ -565,7 +581,7 @@
         compiler_params=params,
         cost_estimate=cost,
         name="relax",
-    )(p, own, fh, fl, c, meta, xy, zd, zu)
+    )(p, own, fh, fl, c, meta, xy, z1, z2)
     slots = lax.all_to_all(slots, ("gx", "gy", "gz"), 0, 0, tiled=True)
     second, rs, oh = pl.pallas_call(
         functools.partial(second_kernel, sizes, dims),
@@ -580,12 +596,12 @@
             pltpu.VMEM((DOFS, DOFS), F32),
             pltpu.VMEM((3 * LANES, DOFS), F32),
             pltpu.VMEM((DOFS, 3 * LANES), F32),
-            pltpu.SemaphoreType.DMA((8,)),
+            pltpu.SemaphoreType.DMA((3,)),
         ],
         compiler_params=params,
         cost_estimate=cost,
         name="second",
-    )(*far(flat, smoother, lift), uh, ul, tr, d, meta, rt, xy, zd, zu)
+    )(*far(flat, smoother, lift), uh, ul, tr, d, meta, rt, xy, z1, z2)
     out = pl.pallas_call(
         correct_kernel,
         out_shape=shape((DOFS, DOFS), F32),

time: 35.2 us -> 32.4 us (0.920)
  starting transfers between devices: 16.3 us -> 14.4 us
  Pallas kernels: 15.6 us -> 14.5 us
    all_to_all x1, starting transfers between devices: 5.32 us -> 4.08 us  [shards(): slots = lax.all_to_all(slots, ('gx', 'gy', 'gz'), 0, 0, tiled=True)]
    pallas_call x1, Pallas kernels: 4.97 us -> 4.26 us  [shards(): pl.pallas_call(functools.partial(smooth_kernel, sizes), out_shape=(split,...]
    ppermute x2, starting transfers between devices: 5.83 us -> 5.12 us  [the longest x1 4.47 us: shards(): z2 = lax.ppermute(z2, 'gz', swaps(0))]
  transfers between devices with their start and end apart: 4 -> 4, of which waited for: 1 -> 1; matrix products, arithmetic and copies ran while one was open for 0% -> 0% of each run, Pallas kernels for 22% -> 23%
where the time goes in v2:
time: 32.4 us; the launch traced here: 32.1 us
  Pallas kernels  14.5 us (45%)
  starting transfers between devices  14.4 us (44%)
  waiting for transfers between devices  3.07 us (9%)
    all_to_all x1, starting transfers between devices, shards(): xy = lax.all_to_all(xy, ('gx', 'gy'), 0, 0, tiled=True)  5.18 us
    ppermute x1, starting transfers between devices, shards(): z2 = lax.ppermute(z2, 'gz', swaps(0))  4.47 us
    pallas_call x1, Pallas kernels, shards(): pl.pallas_call(functools.partial(smooth_kernel, sizes), out_shape=(split,...  4.26 us
    pallas_call x1, Pallas kernels, shards(): pl.pallas_call(functools.partial(second_kernel, sizes, dims), out_shape=(...  4.2 us
    all_to_all x1, starting transfers between devices, shards(): slots = lax.all_to_all(slots, ('gx', 'gy', 'gz'), 0, 0, tiled=True)  4.08 us
    pallas_call x1, Pallas kernels, shards(): pl.pallas_call(functools.partial(prepare_kernel, dims), out_shape=(shape(...  3.1 us
    all_to_all x1, waiting for transfers between devices, shards(): slots = lax.all_to_all(slots, ('gx', 'gy', 'gz'), 0, 0, tiled=True)  3.06 us
    pallas_call x1, Pallas kernels, shards(): pl.pallas_call(functools.partial(relax_kernel, sizes, dims), out_shape=sh...  1.52 us
  transfers between devices with their start and end apart: 4, of which 1 were waited for; matrix products, arithmetic and copies ran while one was open for 0% of the time, Pallas kernels for 23%

profile of v2, /device:TPU:0, one launch (start us, length us, event | category | flops | bytes accessed | tf_op | source)
XLA Modules:
  0.0 32.1 jit_solution(9326349631704379049)
XLA Ops:
  0.0 4.3 %smooth.1 = (bf16[512,512]{1,0:T(8,128)(2,1)S(1)}, bf16[512,512]{1,0:T(8,128)(2,1)S(1)}, bf16[512,512]{1,0:T(8,128)(2,1)S(1)}, bf16[512,512]{1,0:T(8,128)(2,1)S(...) custom-call(f32[512,512]{1,0:T(8,128)} %bitcast.3, ...), custom_call_target="tpu_custom_call" | custom-call | flops 2000000000 | bytes 4194304 | tf_op jit(solution)/shard_map/smooth/pallas_call | solution.py:524
  4.3 5.2 %all-to-all-start = ((f32[8,72,128]{2,1,0:T(8,128)}), f32[8,72,128]{2,1,0:T(8,128)S(1)}, u32[]{:S(2)}, u32[]{:S(2)}) async-start(f32[8,72,128]{2,1,0:T(8,128)} %get-tuple-element.34), calls=%async_computation | async-start | bytes 589824 | tf_op jit(solution)/shard_map/all_to_all | solution.py:559
  9.4 0.6 %collective-permute-start = (f32[16,128]{1,0:T(8,128)S(1)}, f32[16,128]{1,0:T(8,128)S(1)}, u32[]{:S(2)}, u32[]{:S(2)}) collective-permute-start(f32[16,128]{1,0:T(8,128)S(1)} %get-tuple-element.35), channel_id=1, source_target_pairs={{1,2},{2,1},{5,6},{6,5},{9,10},{10,9},{13,14},{14,13},{17,18},{18,... | collective-permute-start | bytes 24584 | tf_op jit(solution)/shard_map/ppermute | solution.py:557
  10.1 4.5 %collective-permute-start.1 = (f32[16,128]{1,0:T(8,128)S(1)}, f32[16,128]{1,0:T(8,128)S(1)}, u32[]{:S(2)}, u32[]{:S(2)}) collective-permute-start(f32[16,128]{1,0:T(8,128)S(1)} %get-tuple-element.36), channel_id=1, source_target_pairs={{0,1},{2,3},{1,0},{3,2},{4,5},{6,7},{5,4},{7,6},{8,9},{10,11},{9,8... | collective-permute-start | bytes 24584 | tf_op jit(solution)/shard_map/ppermute | solution.py:558
  14.6 3.1 %prepare.1 = (f32[64,512]{1,0:T(8,128)S(1)}, f32[8,512]{1,0:T(8,128)S(1)}, bf16[64,384]{1,0:T(8,128)(2,1)S(1)}, bf16[64,384]{1,0:T(8,128)(2,1)S(1)}, f32[4,128]{1,0:T(4,128)S(1)}) custom-call(f32[384,512]{1,0:T(8,128)} %l_hbm.3, f32[512,512]{1,0:T(8,128)} %m_hbm.1, bf16[512,512]{1,0:T(8,128)(2,1)S(1)} %get-tuple-element.25.uh_ref, ...), custom_call_target="tpu_custom_call" | custom-call | flops 2000000000 | bytes 4194304 | tf_op jit(solution)/shard_map/prepare/pallas_call | solution.py:560
  17.7 0.0 collective-permute-done.z1_ref
  17.7 0.0 collective-permute-done.1.z2_ref
  17.7 0.0 all-to-all-done.xy_ref
  17.7 1.5 %relax.1 = f32[32,4,128]{2,1,0:T(4,128)} custom-call(f32[64,512]{1,0:T(8,128)S(1)} %get-tuple-element.38.p_ref, f32[8,512]{1,0:T(8,128)S(1)} %get-tuple-element.39.own_ref, bf16[64,384]{1,0:T(8,128)(2,1)S(1)} %get-tuple-element.40.qh_ref, bf16[64,384]{1,0:T(8,128)(2,1)S(1)} %get-tuple-element.41.ql_ref, f32[8,8]{1,0:T(8,128)S(1)} %get-tuple-element.42.c_ref, ...), custom_call_target="tpu_custom_call" | custom-call | flops 2000000000 | bytes 4194304 | tf_op jit(solution)/shard_map/relax/pallas_call | solution.py:574
  19.2 4.1 %all-to-all-start.1 = ((f32[32,4,128]{2,1,0:T(4,128)}), f32[32,4,128]{2,1,0:T(4,128)S(1)}, u32[]{:S(2)}, u32[]{:S(2)}) async-start(f32[32,4,128]{2,1,0:T(4,128)} %relax.1), calls=%async_computation.1 | async-start | bytes 131072 | tf_op jit(solution)/shard_map/all_to_all | solution.py:585
  23.3 4.2 %second.1 = (f32[512,512]{1,0:T(8,128)S(1)}, bf16[32,512]{1,0:T(8,128)(2,1)S(1)}, bf16[512,128]{1,0:T(8,128)(2,1)S(1)}) custom-call(f32[512,512]{1,0:T(8,128)} %bitcast.4, f32[512,512]{1,0:T(8,128)} %s_hbm.3, f32[384,512]{1,0:T(8,128)} %l_hbm.3, bf16[512,512]{1,0:T(8,128)(2,1)S(1)} %get-tuple-element.25.uh_ref, ...), custom_call_target="tpu_custom_call" | custom-call | flops 2000000000 | bytes 4194304 | tf_op jit(solution)/shard_map/second/pallas_call | solution.py:586
  27.5 3.1 %all-to-all-done.1.slots_ref = f32[32,4,128]{2,1,0:T(4,128)S(1)} async-done(((f32[32,4,128]{2,1,0:T(4,128)}), f32[32,4,128]{2,1,0:T(4,128)S(1)}, u32[]{:S(2)}, u32[]{:S(2)}) %all-to-all-start.1) | async-done | bytes 65568 | tf_op jit(solution)/shard_map/all_to_all | solution.py:585
  30.6 1.5 %correct.1 = f32[512,512]{1,0:T(8,128)} custom-call(f32[512,512]{1,0:T(8,128)S(1)} %get-tuple-element.37.second_ref, f32[32,4,128]{2,1,0:T(4,128)S(1)} %all-to-all-done.1.slots_ref, f32[16,128]{1,0:T(8,128)S(1)} %get-tuple-element.33.meta_ref, bf16[512,128]{1,0:T(8,128)(2,1)S(1)} %get-tuple-element.43.oh_ref, bf16[32,512]{1,0:T(8,128)(2,1)S(1)} %get-tuple-element.44.rs_ref), custom_call_target="tpu_custom_call" | custom-call | tf_op jit(solution)/shard_map/correct/pallas_call | solution.py:605
Async XLA Ops:
  4.3 13.4 %all-to-all-start = ((f32[8,72,128]{2,1,0:T(8,128)}), f32[8,72,128]{2,1,0:T(8,128)S(1)}, u32[]{:S(2)}, u32[]{:S(2)}) async-start(f32[8,72,128]{2,1,0:T(8,128)} %get-tuple-element.34), calls=%async_computation | async-start | bytes 589824 | tf_op jit(solution)/shard_map/all_to_all | solution.py:559
  9.4 8.2 %collective-permute-start = (f32[16,128]{1,0:T(8,128)S(1)}, f32[16,128]{1,0:T(8,128)S(1)}, u32[]{:S(2)}, u32[]{:S(2)}) collective-permute-start(f32[16,128]{1,0:T(8,128)S(1)} %get-tuple-element.35), channel_id=1, source_target_pairs={{1,2},{2,1},{5,6},{6,5},{9,10},{10,9},{13,14},{14,13},{17,18},{18,... | collective-permute-start | bytes 24584 | tf_op jit(solution)/shard_map/ppermute | solution.py:557
  10.1 7.6 %collective-permute-start.1 = (f32[16,128]{1,0:T(8,128)S(1)}, f32[16,128]{1,0:T(8,128)S(1)}, u32[]{:S(2)}, u32[]{:S(2)}) collective-permute-start(f32[16,128]{1,0:T(8,128)S(1)} %get-tuple-element.36), channel_id=1, source_target_pairs={{0,1},{2,3},{1,0},{3,2},{4,5},{6,7},{5,4},{7,6},{8,9},{10,11},{9,8... | collective-permute-start | bytes 24584 | tf_op jit(solution)/shard_map/ppermute | solution.py:558
  19.2 11.4 %all-to-all-start.1 = ((f32[32,4,128]{2,1,0:T(4,128)}), f32[32,4,128]{2,1,0:T(4,128)S(1)}, u32[]{:S(2)}, u32[]{:S(2)}) async-start(f32[32,4,128]{2,1,0:T(4,128)} %relax.1), calls=%async_computation.1 | async-start | bytes 131072 | tf_op jit(solution)/shard_map/all_to_all | solution.py:585

commit v3 on v2

--- a/solution.py
+++ b/solution.py
@@ -38,8 +38,8 @@
     return lax.dot_general(a, b, dims, preferred_element_type=F32)
 
 
-def dot3(a, b, dims=(((1,), (0,)), ((), ()))):
-    return dot(a[0], b[0], dims) + (dot(a[0], b[1], dims) + dot(a[1], b[0], dims))
+def dot3(a, b):
+    return dot(jnp.concatenate([a[0], a[0], a[1]], 1), jnp.concatenate([b[0], b[1], b[0]], 0))
 
 
 def dot3_few(a, b):
@@ -112,10 +112,10 @@
     return halves(jnp.where(row == lane((n, DOFS)), 1.0, 0.0) - s_ref[part])
 
 
-def start_all(pairs, sems, second=()):
+def start_all(pairs, sems):
     copies = [pltpu.make_async_copy(src, dst, sems.at[i]) for i, (src, dst) in enumerate(pairs)]
-    for i, copy in enumerate(copies):
-        copy.start(priority=1 if i in second else 0)
+    for copy in copies:
+        copy.start()
     return copies
 
 
@@ -126,8 +126,7 @@
         pairs["m"].append((m[0].at[block, block], m[1].at[i]))
     counts = [len(pairs[name]) for name in names]
     first = [sum(counts[:i]) for i in range(len(names))]
-    second = first[names.index("rhs")] if "rhs" in names else -1
-    copies = start_all([pair for name in names for pair in pairs[name]], sems, [second])
+    copies = start_all([pair for name in names for pair in pairs[name]], sems)
 
     def wait(name):
         i = names.index(name)

time: 32.4 us -> 32.4 us (level)
  no operation moved by 1% of the time
where the time goes in v3:
time: 32.4 us; the launch traced here: 32 us
  Pallas kernels  14.7 us (45%)
  starting transfers between devices  14.4 us (44%)
  waiting for transfers between devices  2.92 us (9%)
    all_to_all x1, starting transfers between devices, shards(): xy = lax.all_to_all(xy, ('gx', 'gy'), 0, 0, tiled=True)  5.18 us
    ppermute x1, starting transfers between devices, shards(): z2 = lax.ppermute(z2, 'gz', swaps(0))  4.46 us
    pallas_call x1, Pallas kernels, shards(): pl.pallas_call(functools.partial(second_kernel, sizes, dims), out_shape=(...  4.36 us
    pallas_call x1, Pallas kernels, shards(): pl.pallas_call(functools.partial(smooth_kernel, sizes), out_shape=(split,...  4.23 us
    all_to_all x1, starting transfers between devices, shards(): slots = lax.all_to_all(slots, ('gx', 'gy', 'gz'), 0, 0, tiled=True)  4.07 us
    pallas_call x1, Pallas kernels, shards(): pl.pallas_call(functools.partial(prepare_kernel, dims), out_shape=(shape(...  3.11 us
    all_to_all x1, waiting for transfers between devices, shards(): slots = lax.all_to_all(slots, ('gx', 'gy', 'gz'), 0, 0, tiled=True)  2.91 us
    pallas_call x1, Pallas kernels, shards(): pl.pallas_call(functools.partial(relax_kernel, sizes, dims), out_shape=sh...  1.52 us
  transfers between devices with their start and end apart: 4, of which 1 were waited for; matrix products, arithmetic and copies ran while one was open for 0% of the time, Pallas kernels for 23%

profile of v3, /device:TPU:0, one launch (start us, length us, event | category | flops | bytes accessed | tf_op | source)
XLA Modules:
  0.0 32.0 jit_solution(6472161044824006516)
XLA Ops:
  0.0 4.2 %smooth.1 = (bf16[512,512]{1,0:T(8,128)(2,1)S(1)}, bf16[512,512]{1,0:T(8,128)(2,1)S(1)}, bf16[512,512]{1,0:T(8,128)(2,1)S(1)}, bf16[512,512]{1,0:T(8,128)(2,1)S(...) custom-call(f32[512,512]{1,0:T(8,128)} %bitcast.3, ...), custom_call_target="tpu_custom_call" | custom-call | flops 2000000000 | bytes 4194304 | tf_op jit(solution)/shard_map/smooth/pallas_call | solution.py:523
  4.2 5.2 %all-to-all-start = ((f32[8,72,128]{2,1,0:T(8,128)}), f32[8,72,128]{2,1,0:T(8,128)S(1)}, u32[]{:S(2)}, u32[]{:S(2)}) async-start(f32[8,72,128]{2,1,0:T(8,128)} %get-tuple-element.34), calls=%async_computation | async-start | bytes 589824 | tf_op jit(solution)/shard_map/all_to_all | solution.py:558
  9.4 0.6 %collective-permute-start = (f32[16,128]{1,0:T(8,128)S(1)}, f32[16,128]{1,0:T(8,128)S(1)}, u32[]{:S(2)}, u32[]{:S(2)}) collective-permute-start(f32[16,128]{1,0:T(8,128)S(1)} %get-tuple-element.35), channel_id=1, source_target_pairs={{1,2},{2,1},{5,6},{6,5},{9,10},{10,9},{13,14},{14,13},{17,18},{18,... | collective-permute-start | bytes 24584 | tf_op jit(solution)/shard_map/ppermute | solution.py:556
  10.1 4.5 %collective-permute-start.1 = (f32[16,128]{1,0:T(8,128)S(1)}, f32[16,128]{1,0:T(8,128)S(1)}, u32[]{:S(2)}, u32[]{:S(2)}) collective-permute-start(f32[16,128]{1,0:T(8,128)S(1)} %get-tuple-element.36), channel_id=1, source_target_pairs={{0,1},{2,3},{1,0},{3,2},{4,5},{6,7},{5,4},{7,6},{8,9},{10,11},{9,8... | collective-permute-start | bytes 24584 | tf_op jit(solution)/shard_map/ppermute | solution.py:557
  14.5 3.1 %prepare.1 = (f32[64,512]{1,0:T(8,128)S(1)}, f32[8,512]{1,0:T(8,128)S(1)}, bf16[64,384]{1,0:T(8,128)(2,1)S(1)}, bf16[64,384]{1,0:T(8,128)(2,1)S(1)}, f32[4,128]{1,0:T(4,128)S(1)}) custom-call(f32[384,512]{1,0:T(8,128)} %l_hbm.3, f32[512,512]{1,0:T(8,128)} %m_hbm.1, bf16[512,512]{1,0:T(8,128)(2,1)S(1)} %get-tuple-element.25.uh_ref, ...), custom_call_target="tpu_custom_call" | custom-call | flops 2000000000 | bytes 4194304 | tf_op jit(solution)/shard_map/prepare/pallas_call | solution.py:559
  17.7 0.0 collective-permute-done.z1_ref
  17.7 0.0 collective-permute-done.1.z2_ref
  17.7 0.0 all-to-all-done.xy_ref
  17.7 1.5 %relax.1 = f32[32,4,128]{2,1,0:T(4,128)} custom-call(f32[64,512]{1,0:T(8,128)S(1)} %get-tuple-element.38.p_ref, f32[8,512]{1,0:T(8,128)S(1)} %get-tuple-element.39.own_ref, bf16[64,384]{1,0:T(8,128)(2,1)S(1)} %get-tuple-element.40.qh_ref, bf16[64,384]{1,0:T(8,128)(2,1)S(1)} %get-tuple-element.41.ql_ref, f32[8,8]{1,0:T(8,128)S(1)} %get-tuple-element.42.c_ref, ...), custom_call_target="tpu_custom_call" | custom-call | flops 2000000000 | bytes 4194304 | tf_op jit(solution)/shard_map/relax/pallas_call | solution.py:573
  19.2 4.1 %all-to-all-start.1 = ((f32[32,4,128]{2,1,0:T(4,128)}), f32[32,4,128]{2,1,0:T(4,128)S(1)}, u32[]{:S(2)}, u32[]{:S(2)}) async-start(f32[32,4,128]{2,1,0:T(4,128)} %relax.1), calls=%async_computation.1 | async-start | bytes 131072 | tf_op jit(solution)/shard_map/all_to_all | solution.py:584
  23.3 4.4 %second.1 = (f32[512,512]{1,0:T(8,128)S(1)}, bf16[32,512]{1,0:T(8,128)(2,1)S(1)}, bf16[512,128]{1,0:T(8,128)(2,1)S(1)}) custom-call(f32[512,512]{1,0:T(8,128)} %bitcast.4, f32[512,512]{1,0:T(8,128)} %s_hbm.3, f32[384,512]{1,0:T(8,128)} %l_hbm.3, bf16[512,512]{1,0:T(8,128)(2,1)S(1)} %get-tuple-element.25.uh_ref, ...), custom_call_target="tpu_custom_call" | custom-call | flops 2000000000 | bytes 4194304 | tf_op jit(solution)/shard_map/second/pallas_call | solution.py:585
  27.7 2.9 %all-to-all-done.1.slots_ref = f32[32,4,128]{2,1,0:T(4,128)S(1)} async-done(((f32[32,4,128]{2,1,0:T(4,128)}), f32[32,4,128]{2,1,0:T(4,128)S(1)}, u32[]{:S(2)}, u32[]{:S(2)}) %all-to-all-start.1) | async-done | bytes 65568 | tf_op jit(solution)/shard_map/all_to_all | solution.py:584
  30.6 1.5 %correct.1 = f32[512,512]{1,0:T(8,128)} custom-call(f32[512,512]{1,0:T(8,128)S(1)} %get-tuple-element.37.second_ref, f32[32,4,128]{2,1,0:T(4,128)S(1)} %all-to-all-done.1.slots_ref, f32[16,128]{1,0:T(8,128)S(1)} %get-tuple-element.33.meta_ref, bf16[512,128]{1,0:T(8,128)(2,1)S(1)} %get-tuple-element.43.oh_ref, bf16[32,512]{1,0:T(8,128)(2,1)S(1)} %get-tuple-element.44.rs_ref), custom_call_target="tpu_custom_call" | custom-call | tf_op jit(solution)/shard_map/correct/pallas_call | solution.py:604
Async XLA Ops:
  4.2 13.4 %all-to-all-start = ((f32[8,72,128]{2,1,0:T(8,128)}), f32[8,72,128]{2,1,0:T(8,128)S(1)}, u32[]{:S(2)}, u32[]{:S(2)}) async-start(f32[8,72,128]{2,1,0:T(8,128)} %get-tuple-element.34), calls=%async_computation | async-start | bytes 589824 | tf_op jit(solution)/shard_map/all_to_all | solution.py:558
  9.4 8.2 %collective-permute-start = (f32[16,128]{1,0:T(8,128)S(1)}, f32[16,128]{1,0:T(8,128)S(1)}, u32[]{:S(2)}, u32[]{:S(2)}) collective-permute-start(f32[16,128]{1,0:T(8,128)S(1)} %get-tuple-element.35), channel_id=1, source_target_pairs={{1,2},{2,1},{5,6},{6,5},{9,10},{10,9},{13,14},{14,13},{17,18},{18,... | collective-permute-start | bytes 24584 | tf_op jit(solution)/shard_map/ppermute | solution.py:556
  10.1 7.6 %collective-permute-start.1 = (f32[16,128]{1,0:T(8,128)S(1)}, f32[16,128]{1,0:T(8,128)S(1)}, u32[]{:S(2)}, u32[]{:S(2)}) collective-permute-start(f32[16,128]{1,0:T(8,128)S(1)} %get-tuple-element.36), channel_id=1, source_target_pairs={{0,1},{2,3},{1,0},{3,2},{4,5},{6,7},{5,4},{7,6},{8,9},{10,11},{9,8... | collective-permute-start | bytes 24584 | tf_op jit(solution)/shard_map/ppermute | solution.py:557
  19.2 11.4 %all-to-all-start.1 = ((f32[32,4,128]{2,1,0:T(4,128)}), f32[32,4,128]{2,1,0:T(4,128)S(1)}, u32[]{:S(2)}, u32[]{:S(2)}) async-start(f32[32,4,128]{2,1,0:T(4,128)} %relax.1), calls=%async_computation.1 | async-start | bytes 131072 | tf_op jit(solution)/shard_map/all_to_all | solution.py:584

commit v4 on v3

--- a/solution.py
+++ b/solution.py
@@ -38,8 +38,8 @@
     return lax.dot_general(a, b, dims, preferred_element_type=F32)
 
 
-def dot3(a, b):
-    return dot(jnp.concatenate([a[0], a[0], a[1]], 1), jnp.concatenate([b[0], b[1], b[0]], 0))
+def dot3(a, b, dims=(((1,), (0,)), ((), ()))):
+    return dot(a[0], b[0], dims) + (dot(a[0], b[1], dims) + dot(a[1], b[0], dims))
 
 
 def dot3_few(a, b):
@@ -151,8 +151,8 @@
 
 
 def smooth_kernel(sizes, rhs_hbm, s_hbm, coef_hbm, lab_hbm, rt_hbm, c_hbm,
-                  uh_ref, ul_ref, th_ref, nh_ref, tr_ref, meta_ref, xy_ref, z1_ref, z2_ref, rt_ref, c_ref, rn_ref,
-                  rhs_ref, s_ref, coef_ref, lab_ref, t_ref, sems):
+                  uh_ref, ul_ref, th_ref, nh_ref, tr_ref, meta_ref, xy_hbm, z1_ref, z2_ref, rt_ref, c_ref, rn_ref,
+                  rhs_ref, s_ref, coef_ref, lab_ref, t_ref, nl_ref, out_ref, sems, out_sems):
     ngx, ngy, ngz = sizes
     gx, gy, gz = position(sizes)
     half = DOFS // 2
@@ -180,13 +180,21 @@
     meta_ref[META : META + ex] = cell_rows(coef_ref)
     rc = reciprocal(meta_ref[META : META + ex])
 
-    rt = halves(rt_ref[...])
-
     def near_part(part):
         near = near_identity(s_ref, part)
-        nh_ref[part] = near[0]
-        rn_ref[:, part] = dot3_few(rt, near)
+        nh_ref[part], nl_ref[part] = near
         return near
+
+    here = gx * ngy + gy
+    outs = []
+
+    def send(i, there, slot, packed):
+        n = packed.shape[0]
+        out_ref[i, :n] = packed
+        out_ref[i, n:] = meta
+        out = pltpu.make_async_copy(out_ref.at[i], xy_hbm.at[jnp.where(there, slot, here)], out_sems.at[i])
+        pl.when(there)(out.start)
+        outs.append((there, out))
 
     wait(4, 2)
     near = near_part(blocks[0])
@@ -205,6 +213,8 @@
         pairs.append(traces(u, split, pick, rc[rows]))
         for i, pair in enumerate(pairs[-1]):
             tr_ref[rows, i * LANES : (i + 1) * LANES] = pair
+        if rows is blocks[0]:
+            send(0, gx > 0, here - ngy, pack0(pairs[0][0][:plane]))
     x_pair, y_pair, z_pair = [jnp.concatenate([block[i] for block in pairs], 0) for i in range(3)]
 
     def y_rows(y):
@@ -215,20 +225,16 @@
     def z_rows(z):
         return jnp.concatenate([z_pair[i * ez + z : i * ez + z + 1] for i in range(ex * ey)], 0)
 
-    def send(ref, slot, payload):
-        n = payload.shape[0]
-        ref[slot, :n] = payload
-        ref[slot, n:] = meta
-
-    here = gx * ngy + gy
-    send(xy_ref, jnp.where(gx < ngx - 1, here + ngy, here), pack7(x_pair[(ex - 1) * plane :]))
-    send(xy_ref, jnp.where(gx > 0, here - ngy, here), pack0(x_pair[:plane]))
-    send(xy_ref, jnp.where(gy < ngy - 1, here + 1, here), pack7(y_rows(ey - 1)))
-    send(xy_ref, jnp.where(gy > 0, here - 1, here), pack0(y_rows(0)))
+    send(1, gx < ngx - 1, here + ngy, pack7(x_pair[(ex - 1) * plane :]))
+    send(2, gy < ngy - 1, here + 1, pack7(y_rows(ey - 1)))
+    send(3, gy > 0, here - 1, pack0(y_rows(0)))
+    rn_ref[...] = dot3_few(halves(rt_ref[...]), (nh_ref[...], nl_ref[...]))
     odd = lax.rem(gz, 2) == 1
     up, down = pack7(z_rows(ez - 1)), pack0(z_rows(0))
     z1_ref[...] = jnp.concatenate([jnp.where(odd, up, down), meta], 0)
     z2_ref[...] = jnp.concatenate([jnp.where(odd, down, up), meta], 0)
+    for there, out in outs:
+        pl.when(there)(out.wait)
 
 
 def receive(sizes, dims, xy_ref, z1_ref, z2_ref):
@@ -335,7 +341,7 @@
 
 
 def relax_kernel(sizes, dims, p_ref, own_ref, qh_ref, ql_ref, c_ref, meta_ref, xy_ref, z1_ref, z2_ref,
-                 slots_ref, f_ref, bins_ref):
+                 slots_hbm, f_ref, bins_ref, sem):
     ngx, ngy, ngz = sizes
     gx, gy, gz = position(sizes)
     ex, ey, ez = dims
@@ -429,7 +435,7 @@
         packed(mixed[:, i * FACE : (i + 1) * FACE]) for i in range(len(blocks))
     ]
 
-    count = slots_ref.shape[0]
+    count = slots_hbm.shape[0]
     bins_ref[...] = jnp.zeros_like(bins_ref)
 
     def put(dx, dy, dz, share):
@@ -456,7 +462,9 @@
     put(gx, gy + 1, gz - 1, yu + zd)
     put(gx, gy - 1, gz + 1, yd + zu)
     put(gx, gy - 1, gz - 1, yd + zd)
-    slots_ref[...] = bins_ref[:count]
+    copy = pltpu.make_async_copy(bins_ref.at[pl.ds(0, count)], slots_hbm, sem)
+    copy.start()
+    copy.wait()
 
 
 def second_kernel(sizes, dims, rhs_hbm, s_hbm, l_hbm, uh_ref, ul_ref, tr_ref, d_ref, meta_ref, rt_ref, xy_ref, z1_ref, z2_ref,
@@ -537,13 +545,17 @@
             few,
         ),
         in_specs=[hbm] * 6,
+        out_specs=[vmem] * 6 + [hbm] + [vmem] * 5,
         scratch_shapes=[
             pltpu.VMEM((DOFS, DOFS), F32),
             pltpu.VMEM((DOFS, DOFS), F32),
             pltpu.VMEM(dims, F32),
             pltpu.VMEM(dims, jnp.int32),
             pltpu.VMEM((DOFS, DOFS), F32),
+            pltpu.VMEM((DOFS, DOFS), BF16),
+            pltpu.VMEM((4, face + META, LANES), F32),
             pltpu.SemaphoreType.DMA((12,)),
+            pltpu.SemaphoreType.DMA((4,)),
         ],
         compiler_params=params,
         cost_estimate=cost,
@@ -573,9 +585,11 @@
     slots = pl.pallas_call(
         functools.partial(relax_kernel, sizes, dims),
         out_shape=shape((count, COARSE // 2, LANES), F32),
+        out_specs=hbm,
         scratch_shapes=[
             pltpu.VMEM((DOFS, LANES), F32),
             pltpu.VMEM((count + 1, COARSE // 2, LANES), F32),
+            pltpu.SemaphoreType.DMA,
         ],
         compiler_params=params,
         cost_estimate=cost,

time: 32.4 us -> 32.1 us (level)
  Pallas kernels: 14.7 us -> 14.1 us
    pallas_call x1, Pallas kernels: 4.23 us -> 3.86 us  [shards(): pl.pallas_call(functools.partial(smooth_kernel, sizes), out_shape=(split,...]
where the time goes in v4:
time: 32.1 us; the launch traced here: 31.7 us
  starting transfers between devices  14.4 us (45%)
  Pallas kernels  14.1 us (44%)
  waiting for transfers between devices  3.07 us (10%)
    all_to_all x1, starting transfers between devices, shards(): xy = lax.all_to_all(xy, ('gx', 'gy'), 0, 0, tiled=True)  5.25 us
    ppermute x1, starting transfers between devices, shards(): z2 = lax.ppermute(z2, 'gz', swaps(0))  4.47 us
    pallas_call x1, Pallas kernels, shards(): pl.pallas_call(functools.partial(second_kernel, sizes, dims), out_shape=(...  4.21 us
    all_to_all x1, starting transfers between devices, shards(): slots = lax.all_to_all(slots, ('gx', 'gy', 'gz'), 0, 0, tiled=True)  4.08 us
    pallas_call x1, Pallas kernels, shards(): pl.pallas_call(functools.partial(smooth_kernel, sizes), out_shape=(split,...  3.86 us
    pallas_call x1, Pallas kernels, shards(): pl.pallas_call(functools.partial(prepare_kernel, dims), out_shape=(shape(...  3.1 us
    all_to_all x1, waiting for transfers between devices, shards(): slots = lax.all_to_all(slots, ('gx', 'gy', 'gz'), 0, 0, tiled=True)  3.06 us
    pallas_call x1, Pallas kernels, shards(): pl.pallas_call(functools.partial(relax_kernel, sizes, dims), out_shape=sh...  1.51 us
  transfers between devices with their start and end apart: 4, of which 1 were waited for; matrix products, arithmetic and copies ran while one was open for 0% of the time, Pallas kernels for 23%

profile of v4, /device:TPU:0, one launch (start us, length us, event | category | flops | bytes accessed | tf_op | source)
XLA Modules:
  0.0 31.7 jit_solution(12621493696587306252)
XLA Ops:
  0.0 3.9 %smooth.1 = (bf16[512,512]{1,0:T(8,128)(2,1)S(1)}, bf16[512,512]{1,0:T(8,128)(2,1)S(1)}, bf16[512,512]{1,0:T(8,128)(2,1)S(1)}, bf16[512,512]{1,0:T(8,128)(2,1)S(...) custom-call(f32[512,512]{1,0:T(8,128)} %bitcast.3, ...), custom_call_target="tpu_custom_call" | custom-call | flops 2000000000 | bytes 4194304 | tf_op jit(solution)/shard_map/smooth/pallas_call | solution.py:531
  3.9 5.2 %all-to-all-start = ((f32[8,72,128]{2,1,0:T(8,128)}), f32[8,72,128]{2,1,0:T(8,128)S(1)}, u32[]{:S(2)}, u32[]{:S(2)}) async-start(f32[8,72,128]{2,1,0:T(8,128)} %get-tuple-element.34), calls=%async_computation | async-start | bytes 589824 | tf_op jit(solution)/shard_map/all_to_all | solution.py:570
  9.1 0.6 %collective-permute-start = (f32[16,128]{1,0:T(8,128)S(1)}, f32[16,128]{1,0:T(8,128)S(1)}, u32[]{:S(2)}, u32[]{:S(2)}) collective-permute-start(f32[16,128]{1,0:T(8,128)S(1)} %get-tuple-element.35), channel_id=1, source_target_pairs={{1,2},{2,1},{5,6},{6,5},{9,10},{10,9},{13,14},{14,13},{17,18},{18,... | collective-permute-start | bytes 24584 | tf_op jit(solution)/shard_map/ppermute | solution.py:568
  9.8 4.5 %collective-permute-start.1 = (f32[16,128]{1,0:T(8,128)S(1)}, f32[16,128]{1,0:T(8,128)S(1)}, u32[]{:S(2)}, u32[]{:S(2)}) collective-permute-start(f32[16,128]{1,0:T(8,128)S(1)} %get-tuple-element.36), channel_id=1, source_target_pairs={{0,1},{2,3},{1,0},{3,2},{4,5},{6,7},{5,4},{7,6},{8,9},{10,11},{9,8... | collective-permute-start | bytes 24584 | tf_op jit(solution)/shard_map/ppermute | solution.py:569
  14.2 3.1 %prepare.1 = (f32[64,512]{1,0:T(8,128)S(1)}, f32[8,512]{1,0:T(8,128)S(1)}, bf16[64,384]{1,0:T(8,128)(2,1)S(1)}, bf16[64,384]{1,0:T(8,128)(2,1)S(1)}, f32[4,128]{1,0:T(4,128)S(1)}) custom-call(f32[384,512]{1,0:T(8,128)} %l_hbm.3, f32[512,512]{1,0:T(8,128)} %m_hbm.1, bf16[512,512]{1,0:T(8,128)(2,1)S(1)} %get-tuple-element.25.uh_ref, ...), custom_call_target="tpu_custom_call" | custom-call | flops 2000000000 | bytes 4194304 | tf_op jit(solution)/shard_map/prepare/pallas_call | solution.py:571
  17.3 0.0 collective-permute-done.z1_ref
  17.4 0.0 collective-permute-done.1.z2_ref
  17.4 0.0 all-to-all-done.xy_ref
  17.4 1.5 %relax.1 = f32[32,4,128]{2,1,0:T(4,128)} custom-call(f32[64,512]{1,0:T(8,128)S(1)} %get-tuple-element.38.p_ref, f32[8,512]{1,0:T(8,128)S(1)} %get-tuple-element.39.own_ref, bf16[64,384]{1,0:T(8,128)(2,1)S(1)} %get-tuple-element.40.qh_ref, bf16[64,384]{1,0:T(8,128)(2,1)S(1)} %get-tuple-element.41.ql_ref, f32[8,8]{1,0:T(8,128)S(1)} %get-tuple-element.42.c_ref, ...), custom_call_target="tpu_custom_call" | custom-call | flops 2000000000 | bytes 4194304 | tf_op jit(solution)/shard_map/relax/pallas_call | solution.py:585
  18.9 4.1 %all-to-all-start.1 = ((f32[32,4,128]{2,1,0:T(4,128)}), f32[32,4,128]{2,1,0:T(4,128)S(1)}, u32[]{:S(2)}, u32[]{:S(2)}) async-start(f32[32,4,128]{2,1,0:T(4,128)} %relax.1), calls=%async_computation.1 | async-start | bytes 131072 | tf_op jit(solution)/shard_map/all_to_all | solution.py:598
  23.0 4.2 %second.1 = (f32[512,512]{1,0:T(8,128)S(1)}, bf16[32,512]{1,0:T(8,128)(2,1)S(1)}, bf16[512,128]{1,0:T(8,128)(2,1)S(1)}) custom-call(f32[512,512]{1,0:T(8,128)} %bitcast.4, f32[512,512]{1,0:T(8,128)} %s_hbm.3, f32[384,512]{1,0:T(8,128)} %l_hbm.3, bf16[512,512]{1,0:T(8,128)(2,1)S(1)} %get-tuple-element.25.uh_ref, ...), custom_call_target="tpu_custom_call" | custom-call | flops 2000000000 | bytes 4194304 | tf_op jit(solution)/shard_map/second/pallas_call | solution.py:599
  27.2 3.1 %all-to-all-done.1.slots_ref = f32[32,4,128]{2,1,0:T(4,128)S(1)} async-done(((f32[32,4,128]{2,1,0:T(4,128)}), f32[32,4,128]{2,1,0:T(4,128)S(1)}, u32[]{:S(2)}, u32[]{:S(2)}) %all-to-all-start.1) | async-done | bytes 65568 | tf_op jit(solution)/shard_map/all_to_all | solution.py:598
  30.3 1.5 %correct.1 = f32[512,512]{1,0:T(8,128)} custom-call(f32[512,512]{1,0:T(8,128)S(1)} %get-tuple-element.37.second_ref, f32[32,4,128]{2,1,0:T(4,128)S(1)} %all-to-all-done.1.slots_ref, f32[16,128]{1,0:T(8,128)S(1)} %get-tuple-element.33.meta_ref, bf16[512,128]{1,0:T(8,128)(2,1)S(1)} %get-tuple-element.43.oh_ref, bf16[32,512]{1,0:T(8,128)(2,1)S(1)} %get-tuple-element.44.rs_ref), custom_call_target="tpu_custom_call" | custom-call | tf_op jit(solution)/shard_map/correct/pallas_call | solution.py:618
Async XLA Ops:
  3.9 13.5 %all-to-all-start = ((f32[8,72,128]{2,1,0:T(8,128)}), f32[8,72,128]{2,1,0:T(8,128)S(1)}, u32[]{:S(2)}, u32[]{:S(2)}) async-start(f32[8,72,128]{2,1,0:T(8,128)} %get-tuple-element.34), calls=%async_computation | async-start | bytes 589824 | tf_op jit(solution)/shard_map/all_to_all | solution.py:570
  9.1 8.2 %collective-permute-start = (f32[16,128]{1,0:T(8,128)S(1)}, f32[16,128]{1,0:T(8,128)S(1)}, u32[]{:S(2)}, u32[]{:S(2)}) collective-permute-start(f32[16,128]{1,0:T(8,128)S(1)} %get-tuple-element.35), channel_id=1, source_target_pairs={{1,2},{2,1},{5,6},{6,5},{9,10},{10,9},{13,14},{14,13},{17,18},{18,... | collective-permute-start | bytes 24584 | tf_op jit(solution)/shard_map/ppermute | solution.py:568
  9.8 7.6 %collective-permute-start.1 = (f32[16,128]{1,0:T(8,128)S(1)}, f32[16,128]{1,0:T(8,128)S(1)}, u32[]{:S(2)}, u32[]{:S(2)}) collective-permute-start(f32[16,128]{1,0:T(8,128)S(1)} %get-tuple-element.36), channel_id=1, source_target_pairs={{0,1},{2,3},{1,0},{3,2},{4,5},{6,7},{5,4},{7,6},{8,9},{10,11},{9,8... | collective-permute-start | bytes 24584 | tf_op jit(solution)/shard_map/ppermute | solution.py:569
  18.9 11.4 %all-to-all-start.1 = ((f32[32,4,128]{2,1,0:T(4,128)}), f32[32,4,128]{2,1,0:T(4,128)S(1)}, u32[]{:S(2)}, u32[]{:S(2)}) async-start(f32[32,4,128]{2,1,0:T(4,128)} %relax.1), calls=%async_computation.1 | async-start | bytes 131072 | tf_op jit(solution)/shard_map/all_to_all | solution.py:598

commit v5 on v4

--- a/solution.py
+++ b/solution.py
@@ -107,9 +107,15 @@
 
 
 def near_identity(s_ref, part):
-    n = part.stop - part.start
-    row = lax.broadcasted_iota(jnp.int32, (n, DOFS), 0) + part.start
-    return halves(jnp.where(row == lane((n, DOFS)), 1.0, 0.0) - s_ref[part])
+    diagonal = lax.broadcasted_iota(jnp.int32, (LANES, LANES), 0) == lane((LANES, LANES))
+    identity = jnp.where(diagonal, 1.0, 0.0)
+    rows = []
+    for start in range(part.start, part.stop, LANES):
+        s = s_ref[start : start + LANES]
+        tile = identity - s[:, start : start + LANES]
+        pieces = [-s[:, :start], tile, -s[:, start + LANES :]]
+        rows.append(jnp.concatenate([piece for piece in pieces if piece.shape[1]], 1))
+    return halves(jnp.concatenate(rows, 0))
 
 
 def start_all(pairs, sems):
@@ -174,7 +180,7 @@
     wait(0, 4)
     lab = cell_rows(lab_ref)
     counts = dot(jnp.ones((8, DOFS), BF16), onehot_rows(as_row(lab)), NT)
-    weights = jnp.concatenate([1.0 + counts[0:1], jnp.ones((1, FACE), F32)], 1)
+    weights = 1.0 + jnp.concatenate([counts[0:1], counts[0:1]], 1)
     meta = jnp.concatenate([lab, weights, jnp.zeros((META - 5, LANES), F32)], 0)
     meta_ref[:META] = meta
     meta_ref[META : META + ex] = cell_rows(coef_ref)
@@ -404,7 +410,7 @@
 
     def scatter(values, onehot):
         high, low = halves(values)
-        out = dot(jnp.concatenate([high, low], 0), onehot, NT)
+        out = dot(jnp.concatenate([high, low], 0), jnp.concatenate([onehot, onehot], 0), NT)
         return out[:COARSE] + out[COARSE:]
 
     def shifted(labels, shift, keep):
@@ -421,19 +427,20 @@
         (scatter(p_z7, onehot_rows(shifted(z_up[1], ez - 1, rows % ez == ez - 1))), z_up[2]),
         (scatter(p_z0, onehot_rows(shifted(z_down[1], LANES - ez + 1, rows % ez == 0))), z_down[2]),
     ]
-    raw = jnp.concatenate([z for z, _ in blocks], 1)
-    mixed = raw + raw
-    for k in range(COARSE):
-        mixed = mixed - c_ref[:, k : k + 1] * raw[k : k + 1]
+    columns = [jnp.broadcast_to(c_ref[:, k : k + 1], (COARSE, LANES)) for k in range(COARSE)]
+
+    def mixed(block):
+        out = block + block
+        for k in range(COARSE):
+            out = out - columns[k] * block[k : k + 1]
+        return out
 
     def packed(block):
-        rows = COARSE // 2
-        return jnp.concatenate([block[:rows], block[rows:]], 1)
-
-    b0, xu, xd, yu, yd, zu, zd = [packed(z / w[:, :FACE]) for z, w in blocks]
-    a0, axu, axd, ayu, ayd, azu, azd = [
-        packed(mixed[:, i * FACE : (i + 1) * FACE]) for i in range(len(blocks))
-    ]
+        half = COARSE // 2
+        return jnp.where(lane((half, LANES)) < FACE, block[:half], block[half:])
+
+    b0, xu, xd, yu, yd, zu, zd = [packed(z / w) for z, w in blocks]
+    a0, axu, axd, ayu, ayd, azu, azd = [packed(mixed(z)) for z, _ in blocks]
 
     count = slots_hbm.shape[0]
     bins_ref[...] = jnp.zeros_like(bins_ref)

time: 32.1 us -> 32 us (level)
  no operation moved by 1% of the time
where the time goes in v5:
time: 32 us; the launch traced here: 31.7 us
  starting transfers between devices  14.4 us (45%)
  Pallas kernels  14.1 us (44%)
  waiting for transfers between devices  3.12 us (10%)
    all_to_all x1, starting transfers between devices, shards(): xy = lax.all_to_all(xy, ('gx', 'gy'), 0, 0, tiled=True)  5.24 us
    ppermute x1, starting transfers between devices, shards(): z2 = lax.ppermute(z2, 'gz', swaps(0))  4.47 us
    pallas_call x1, Pallas kernels, shards(): pl.pallas_call(functools.partial(second_kernel, sizes, dims), out_shape=(...  4.15 us
    all_to_all x1, starting transfers between devices, shards(): slots = lax.all_to_all(slots, ('gx', 'gy', 'gz'), 0, 0, tiled=True)  4.06 us
    pallas_call x1, Pallas kernels, shards(): pl.pallas_call(functools.partial(smooth_kernel, sizes), out_shape=(split,...  3.85 us
    all_to_all x1, waiting for transfers between devices, shards(): slots = lax.all_to_all(slots, ('gx', 'gy', 'gz'), 0, 0, tiled=True)  3.11 us
    pallas_call x1, Pallas kernels, shards(): pl.pallas_call(functools.partial(prepare_kernel, dims), out_shape=(shape(...  3.11 us
    pallas_call x1, Pallas kernels, shards(): pl.pallas_call(correct_kernel, out_shape=shape((DOFS, DOFS), F32), out_sp...  1.47 us
  transfers between devices with their start and end apart: 4, of which 1 were waited for; matrix products, arithmetic and copies ran while one was open for 0% of the time, Pallas kernels for 23%

profile of v5, /device:TPU:0, one launch (start us, length us, event | category | flops | bytes accessed | tf_op | source)
XLA Modules:
  0.0 31.7 jit_solution(13620253950169385823)
XLA Ops:
  0.0 3.8 %smooth.1 = (bf16[512,512]{1,0:T(8,128)(2,1)S(1)}, bf16[512,512]{1,0:T(8,128)(2,1)S(1)}, bf16[512,512]{1,0:T(8,128)(2,1)S(1)}, bf16[512,512]{1,0:T(8,128)(2,1)S(...) custom-call(f32[512,512]{1,0:T(8,128)} %bitcast.3, ...), custom_call_target="tpu_custom_call" | custom-call | flops 2000000000 | bytes 4194304 | tf_op jit(solution)/shard_map/smooth/pallas_call | solution.py:538
  3.9 5.2 %all-to-all-start = ((f32[8,72,128]{2,1,0:T(8,128)}), f32[8,72,128]{2,1,0:T(8,128)S(1)}, u32[]{:S(2)}, u32[]{:S(2)}) async-start(f32[8,72,128]{2,1,0:T(8,128)} %get-tuple-element.34), calls=%async_computation | async-start | bytes 589824 | tf_op jit(solution)/shard_map/all_to_all | solution.py:577
  9.1 0.6 %collective-permute-start = (f32[16,128]{1,0:T(8,128)S(1)}, f32[16,128]{1,0:T(8,128)S(1)}, u32[]{:S(2)}, u32[]{:S(2)}) collective-permute-start(f32[16,128]{1,0:T(8,128)S(1)} %get-tuple-element.35), channel_id=1, source_target_pairs={{1,2},{2,1},{5,6},{6,5},{9,10},{10,9},{13,14},{14,13},{17,18},{18,... | collective-permute-start | bytes 24584 | tf_op jit(solution)/shard_map/ppermute | solution.py:575
  9.8 4.5 %collective-permute-start.1 = (f32[16,128]{1,0:T(8,128)S(1)}, f32[16,128]{1,0:T(8,128)S(1)}, u32[]{:S(2)}, u32[]{:S(2)}) collective-permute-start(f32[16,128]{1,0:T(8,128)S(1)} %get-tuple-element.36), channel_id=1, source_target_pairs={{0,1},{2,3},{1,0},{3,2},{4,5},{6,7},{5,4},{7,6},{8,9},{10,11},{9,8... | collective-permute-start | bytes 24584 | tf_op jit(solution)/shard_map/ppermute | solution.py:576
  14.2 3.1 %prepare.1 = (f32[64,512]{1,0:T(8,128)S(1)}, f32[8,512]{1,0:T(8,128)S(1)}, bf16[64,384]{1,0:T(8,128)(2,1)S(1)}, bf16[64,384]{1,0:T(8,128)(2,1)S(1)}, f32[4,128]{1,0:T(4,128)S(1)}) custom-call(f32[384,512]{1,0:T(8,128)} %l_hbm.3, f32[512,512]{1,0:T(8,128)} %m_hbm.1, bf16[512,512]{1,0:T(8,128)(2,1)S(1)} %get-tuple-element.25.uh_ref, ...), custom_call_target="tpu_custom_call" | custom-call | flops 2000000000 | bytes 4194304 | tf_op jit(solution)/shard_map/prepare/pallas_call | solution.py:578
  17.3 0.0 collective-permute-done.z1_ref
  17.4 0.0 collective-permute-done.1.z2_ref
  17.4 0.0 all-to-all-done.xy_ref
  17.4 1.5 %relax.1 = f32[32,4,128]{2,1,0:T(4,128)} custom-call(f32[64,512]{1,0:T(8,128)S(1)} %get-tuple-element.38.p_ref, f32[8,512]{1,0:T(8,128)S(1)} %get-tuple-element.39.own_ref, bf16[64,384]{1,0:T(8,128)(2,1)S(1)} %get-tuple-element.40.qh_ref, bf16[64,384]{1,0:T(8,128)(2,1)S(1)} %get-tuple-element.41.ql_ref, f32[8,8]{1,0:T(8,128)S(1)} %get-tuple-element.42.c_ref, ...), custom_call_target="tpu_custom_call" | custom-call | flops 2000000000 | bytes 4194304 | tf_op jit(solution)/shard_map/relax/pallas_call | solution.py:592
  18.9 4.1 %all-to-all-start.1 = ((f32[32,4,128]{2,1,0:T(4,128)}), f32[32,4,128]{2,1,0:T(4,128)S(1)}, u32[]{:S(2)}, u32[]{:S(2)}) async-start(f32[32,4,128]{2,1,0:T(4,128)} %relax.1), calls=%async_computation.1 | async-start | bytes 131072 | tf_op jit(solution)/shard_map/all_to_all | solution.py:605
  22.9 4.2 %second.1 = (f32[512,512]{1,0:T(8,128)S(1)}, bf16[32,512]{1,0:T(8,128)(2,1)S(1)}, bf16[512,128]{1,0:T(8,128)(2,1)S(1)}) custom-call(f32[512,512]{1,0:T(8,128)} %bitcast.4, f32[512,512]{1,0:T(8,128)} %s_hbm.3, f32[384,512]{1,0:T(8,128)} %l_hbm.3, bf16[512,512]{1,0:T(8,128)(2,1)S(1)} %get-tuple-element.25.uh_ref, ...), custom_call_target="tpu_custom_call" | custom-call | flops 2000000000 | bytes 4194304 | tf_op jit(solution)/shard_map/second/pallas_call | solution.py:606
  27.1 3.1 %all-to-all-done.1.slots_ref = f32[32,4,128]{2,1,0:T(4,128)S(1)} async-done(((f32[32,4,128]{2,1,0:T(4,128)}), f32[32,4,128]{2,1,0:T(4,128)S(1)}, u32[]{:S(2)}, u32[]{:S(2)}) %all-to-all-start.1) | async-done | bytes 65568 | tf_op jit(solution)/shard_map/all_to_all | solution.py:605
  30.2 1.5 %correct.1 = f32[512,512]{1,0:T(8,128)} custom-call(f32[512,512]{1,0:T(8,128)S(1)} %get-tuple-element.37.second_ref, f32[32,4,128]{2,1,0:T(4,128)S(1)} %all-to-all-done.1.slots_ref, f32[16,128]{1,0:T(8,128)S(1)} %get-tuple-element.33.meta_ref, bf16[512,128]{1,0:T(8,128)(2,1)S(1)} %get-tuple-element.43.oh_ref, bf16[32,512]{1,0:T(8,128)(2,1)S(1)} %get-tuple-element.44.rs_ref), custom_call_target="tpu_custom_call" | custom-call | tf_op jit(solution)/shard_map/correct/pallas_call | solution.py:625
Async XLA Ops:
  3.9 13.5 %all-to-all-start = ((f32[8,72,128]{2,1,0:T(8,128)}), f32[8,72,128]{2,1,0:T(8,128)S(1)}, u32[]{:S(2)}, u32[]{:S(2)}) async-start(f32[8,72,128]{2,1,0:T(8,128)} %get-tuple-element.34), calls=%async_computation | async-start | bytes 589824 | tf_op jit(solution)/shard_map/all_to_all | solution.py:577
  9.1 8.3 %collective-permute-start = (f32[16,128]{1,0:T(8,128)S(1)}, f32[16,128]{1,0:T(8,128)S(1)}, u32[]{:S(2)}, u32[]{:S(2)}) collective-permute-start(f32[16,128]{1,0:T(8,128)S(1)} %get-tuple-element.35), channel_id=1, source_target_pairs={{1,2},{2,1},{5,6},{6,5},{9,10},{10,9},{13,14},{14,13},{17,18},{18,... | collective-permute-start | bytes 24584 | tf_op jit(solution)/shard_map/ppermute | solution.py:575
  9.8 7.6 %collective-permute-start.1 = (f32[16,128]{1,0:T(8,128)S(1)}, f32[16,128]{1,0:T(8,128)S(1)}, u32[]{:S(2)}, u32[]{:S(2)}) collective-permute-start(f32[16,128]{1,0:T(8,128)S(1)} %get-tuple-element.36), channel_id=1, source_target_pairs={{0,1},{2,3},{1,0},{3,2},{4,5},{6,7},{5,4},{7,6},{8,9},{10,11},{9,8... | collective-permute-start | bytes 24584 | tf_op jit(solution)/shard_map/ppermute | solution.py:576
  18.9 11.3 %all-to-all-start.1 = ((f32[32,4,128]{2,1,0:T(4,128)}), f32[32,4,128]{2,1,0:T(4,128)S(1)}, u32[]{:S(2)}, u32[]{:S(2)}) async-start(f32[32,4,128]{2,1,0:T(4,128)} %relax.1), calls=%async_computation.1 | async-start | bytes 131072 | tf_op jit(solution)/shard_map/all_to_all | solution.py:605

commit v6 on v5

--- a/solution.py
+++ b/solution.py
@@ -204,21 +204,22 @@
 
     wait(4, 2)
     near = near_part(blocks[0])
-    wait(6, 2)
-    t_ref[...] = dot3(halves(rhs_ref[:, blocks[0]]), near)
+    for i, rows in enumerate(blocks):
+        wait(6 + i, 1)
+        t_ref[rows] = dot3(halves(rhs_ref[rows, blocks[0]]), near)
     wait(8, 2)
     near = near_part(blocks[1])
-    wait(10, 2)
     pairs = []
-    for rows in blocks:
+    for i, rows in enumerate(blocks):
+        wait(10 + i, 1)
         t = t_ref[rows] + dot3(halves(rhs_ref[rows, blocks[1]]), near)
         th_ref[rows] = t.astype(BF16)
         u = rhs_ref[rows] - t
         split = halves(u)
         uh_ref[rows], ul_ref[rows] = split
         pairs.append(traces(u, split, pick, rc[rows]))
-        for i, pair in enumerate(pairs[-1]):
-            tr_ref[rows, i * LANES : (i + 1) * LANES] = pair
+        for j, pair in enumerate(pairs[-1]):
+            tr_ref[rows, j * LANES : (j + 1) * LANES] = pair
         if rows is blocks[0]:
             send(0, gx > 0, here - ngy, pack0(pairs[0][0][:plane]))
     x_pair, y_pair, z_pair = [jnp.concatenate([block[i] for block in pairs], 0) for i in range(3)]

time: 32 us -> 32.2 us (level)
  no operation moved by 1% of the time
where the time goes in v6:
time: 32.2 us; the launch traced here: 31.9 us
  starting transfers between devices  14.4 us (45%)
  Pallas kernels  14.2 us (44%)
  waiting for transfers between devices  3.12 us (10%)
    all_to_all x1, starting transfers between devices, shards(): xy = lax.all_to_all(xy, ('gx', 'gy'), 0, 0, tiled=True)  5.25 us
    ppermute x1, starting transfers between devices, shards(): z2 = lax.ppermute(z2, 'gz', swaps(0))  4.47 us
    pallas_call x1, Pallas kernels, shards(): pl.pallas_call(functools.partial(second_kernel, sizes, dims), out_shape=(...  4.15 us
    all_to_all x1, starting transfers between devices, shards(): slots = lax.all_to_all(slots, ('gx', 'gy', 'gz'), 0, 0, tiled=True)  4.08 us
    pallas_call x1, Pallas kernels, shards(): pl.pallas_call(functools.partial(smooth_kernel, sizes), out_shape=(split,...  4.05 us
    all_to_all x1, waiting for transfers between devices, shards(): slots = lax.all_to_all(slots, ('gx', 'gy', 'gz'), 0, 0, tiled=True)  3.11 us
    pallas_call x1, Pallas kernels, shards(): pl.pallas_call(functools.partial(prepare_kernel, dims), out_shape=(shape(...  3.11 us
    pallas_call x1, Pallas kernels, shards(): pl.pallas_call(correct_kernel, out_shape=shape((DOFS, DOFS), F32), out_sp...  1.47 us
  transfers between devices with their start and end apart: 4, of which 1 were waited for; matrix products, arithmetic and copies ran while one was open for 0% of the time, Pallas kernels for 23%

profile of v6, /device:TPU:0, one launch (start us, length us, event | category | flops | bytes accessed | tf_op | source)
XLA Modules:
  0.0 31.9 jit_solution(15927006625496802467)
XLA Ops:
  0.0 4.1 %smooth.1 = (bf16[512,512]{1,0:T(8,128)(2,1)S(1)}, bf16[512,512]{1,0:T(8,128)(2,1)S(1)}, bf16[512,512]{1,0:T(8,128)(2,1)S(1)}, bf16[512,512]{1,0:T(8,128)(2,1)S(...) custom-call(f32[512,512]{1,0:T(8,128)} %bitcast.3, ...), custom_call_target="tpu_custom_call" | custom-call | flops 2000000000 | bytes 4194304 | tf_op jit(solution)/shard_map/smooth/pallas_call | solution.py:539
  4.1 5.2 %all-to-all-start = ((f32[8,72,128]{2,1,0:T(8,128)}), f32[8,72,128]{2,1,0:T(8,128)S(1)}, u32[]{:S(2)}, u32[]{:S(2)}) async-start(f32[8,72,128]{2,1,0:T(8,128)} %get-tuple-element.34), calls=%async_computation | async-start | bytes 589824 | tf_op jit(solution)/shard_map/all_to_all | solution.py:578
  9.3 0.6 %collective-permute-start = (f32[16,128]{1,0:T(8,128)S(1)}, f32[16,128]{1,0:T(8,128)S(1)}, u32[]{:S(2)}, u32[]{:S(2)}) collective-permute-start(f32[16,128]{1,0:T(8,128)S(1)} %get-tuple-element.35), channel_id=1, source_target_pairs={{1,2},{2,1},{5,6},{6,5},{9,10},{10,9},{13,14},{14,13},{17,18},{18,... | collective-permute-start | bytes 24584 | tf_op jit(solution)/shard_map/ppermute | solution.py:576
  10.0 4.5 %collective-permute-start.1 = (f32[16,128]{1,0:T(8,128)S(1)}, f32[16,128]{1,0:T(8,128)S(1)}, u32[]{:S(2)}, u32[]{:S(2)}) collective-permute-start(f32[16,128]{1,0:T(8,128)S(1)} %get-tuple-element.36), channel_id=1, source_target_pairs={{0,1},{2,3},{1,0},{3,2},{4,5},{6,7},{5,4},{7,6},{8,9},{10,11},{9,8... | collective-permute-start | bytes 24584 | tf_op jit(solution)/shard_map/ppermute | solution.py:577
  14.4 3.1 %prepare.1 = (f32[64,512]{1,0:T(8,128)S(1)}, f32[8,512]{1,0:T(8,128)S(1)}, bf16[64,384]{1,0:T(8,128)(2,1)S(1)}, bf16[64,384]{1,0:T(8,128)(2,1)S(1)}, f32[4,128]{1,0:T(4,128)S(1)}) custom-call(f32[384,512]{1,0:T(8,128)} %l_hbm.3, f32[512,512]{1,0:T(8,128)} %m_hbm.1, bf16[512,512]{1,0:T(8,128)(2,1)S(1)} %get-tuple-element.25.uh_ref, ...), custom_call_target="tpu_custom_call" | custom-call | flops 2000000000 | bytes 4194304 | tf_op jit(solution)/shard_map/prepare/pallas_call | solution.py:579
  17.5 0.0 collective-permute-done.z1_ref
  17.6 0.0 collective-permute-done.1.z2_ref
  17.6 0.0 all-to-all-done.xy_ref
  17.6 1.5 %relax.1 = f32[32,4,128]{2,1,0:T(4,128)} custom-call(f32[64,512]{1,0:T(8,128)S(1)} %get-tuple-element.38.p_ref, f32[8,512]{1,0:T(8,128)S(1)} %get-tuple-element.39.own_ref, bf16[64,384]{1,0:T(8,128)(2,1)S(1)} %get-tuple-element.40.qh_ref, bf16[64,384]{1,0:T(8,128)(2,1)S(1)} %get-tuple-element.41.ql_ref, f32[8,8]{1,0:T(8,128)S(1)} %get-tuple-element.42.c_ref, ...), custom_call_target="tpu_custom_call" | custom-call | flops 2000000000 | bytes 4194304 | tf_op jit(solution)/shard_map/relax/pallas_call | solution.py:593
  19.1 4.1 %all-to-all-start.1 = ((f32[32,4,128]{2,1,0:T(4,128)}), f32[32,4,128]{2,1,0:T(4,128)S(1)}, u32[]{:S(2)}, u32[]{:S(2)}) async-start(f32[32,4,128]{2,1,0:T(4,128)} %relax.1), calls=%async_computation.1 | async-start | bytes 131072 | tf_op jit(solution)/shard_map/all_to_all | solution.py:606
  23.1 4.2 %second.1 = (f32[512,512]{1,0:T(8,128)S(1)}, bf16[32,512]{1,0:T(8,128)(2,1)S(1)}, bf16[512,128]{1,0:T(8,128)(2,1)S(1)}) custom-call(f32[512,512]{1,0:T(8,128)} %bitcast.4, f32[512,512]{1,0:T(8,128)} %s_hbm.3, f32[384,512]{1,0:T(8,128)} %l_hbm.3, bf16[512,512]{1,0:T(8,128)(2,1)S(1)} %get-tuple-element.25.uh_ref, ...), custom_call_target="tpu_custom_call" | custom-call | flops 2000000000 | bytes 4194304 | tf_op jit(solution)/shard_map/second/pallas_call | solution.py:607
  27.3 3.1 %all-to-all-done.1.slots_ref = f32[32,4,128]{2,1,0:T(4,128)S(1)} async-done(((f32[32,4,128]{2,1,0:T(4,128)}), f32[32,4,128]{2,1,0:T(4,128)S(1)}, u32[]{:S(2)}, u32[]{:S(2)}) %all-to-all-start.1) | async-done | bytes 65568 | tf_op jit(solution)/shard_map/all_to_all | solution.py:606
  30.4 1.5 %correct.1 = f32[512,512]{1,0:T(8,128)} custom-call(f32[512,512]{1,0:T(8,128)S(1)} %get-tuple-element.37.second_ref, f32[32,4,128]{2,1,0:T(4,128)S(1)} %all-to-all-done.1.slots_ref, f32[16,128]{1,0:T(8,128)S(1)} %get-tuple-element.33.meta_ref, bf16[512,128]{1,0:T(8,128)(2,1)S(1)} %get-tuple-element.43.oh_ref, bf16[32,512]{1,0:T(8,128)(2,1)S(1)} %get-tuple-element.44.rs_ref), custom_call_target="tpu_custom_call" | custom-call | tf_op jit(solution)/shard_map/correct/pallas_call | solution.py:626
Async XLA Ops:
  4.1 13.5 %all-to-all-start = ((f32[8,72,128]{2,1,0:T(8,128)}), f32[8,72,128]{2,1,0:T(8,128)S(1)}, u32[]{:S(2)}, u32[]{:S(2)}) async-start(f32[8,72,128]{2,1,0:T(8,128)} %get-tuple-element.34), calls=%async_computation | async-start | bytes 589824 | tf_op jit(solution)/shard_map/all_to_all | solution.py:578
  9.3 8.2 %collective-permute-start = (f32[16,128]{1,0:T(8,128)S(1)}, f32[16,128]{1,0:T(8,128)S(1)}, u32[]{:S(2)}, u32[]{:S(2)}) collective-permute-start(f32[16,128]{1,0:T(8,128)S(1)} %get-tuple-element.35), channel_id=1, source_target_pairs={{1,2},{2,1},{5,6},{6,5},{9,10},{10,9},{13,14},{14,13},{17,18},{18,... | collective-permute-start | bytes 24584 | tf_op jit(solution)/shard_map/ppermute | solution.py:576
  10.0 7.6 %collective-permute-start.1 = (f32[16,128]{1,0:T(8,128)S(1)}, f32[16,128]{1,0:T(8,128)S(1)}, u32[]{:S(2)}, u32[]{:S(2)}) collective-permute-start(f32[16,128]{1,0:T(8,128)S(1)} %get-tuple-element.36), channel_id=1, source_target_pairs={{0,1},{2,3},{1,0},{3,2},{4,5},{6,7},{5,4},{7,6},{8,9},{10,11},{9,8... | collective-permute-start | bytes 24584 | tf_op jit(solution)/shard_map/ppermute | solution.py:577
  19.1 11.4 %all-to-all-start.1 = ((f32[32,4,128]{2,1,0:T(4,128)}), f32[32,4,128]{2,1,0:T(4,128)S(1)}, u32[]{:S(2)}, u32[]{:S(2)}) async-start(f32[32,4,128]{2,1,0:T(4,128)} %relax.1), calls=%async_computation.1 | async-start | bytes 131072 | tf_op jit(solution)/shard_map/all_to_all | solution.py:606

commit v7 on v5

--- a/solution.py
+++ b/solution.py
@@ -206,9 +206,8 @@
     near = near_part(blocks[0])
     wait(6, 2)
     t_ref[...] = dot3(halves(rhs_ref[:, blocks[0]]), near)
-    wait(8, 2)
+    wait(8, 4)
     near = near_part(blocks[1])
-    wait(10, 2)
     pairs = []
     for rows in blocks:
         t = t_ref[rows] + dot3(halves(rhs_ref[rows, blocks[1]]), near)

time: 32 us -> 32 us (level)
  no operation moved by 1% of the time
where the time goes in v7:
time: 32 us; the launch traced here: 31.6 us
  starting transfers between devices  14.4 us (45%)
  Pallas kernels  14 us (44%)
  waiting for transfers between devices  3.13 us (10%)
    all_to_all x1, starting transfers between devices, shards(): xy = lax.all_to_all(xy, ('gx', 'gy'), 0, 0, tiled=True)  5.24 us
    ppermute x1, starting transfers between devices, shards(): z2 = lax.ppermute(z2, 'gz', swaps(0))  4.47 us
    pallas_call x1, Pallas kernels, shards(): pl.pallas_call(functools.partial(second_kernel, sizes, dims), out_shape=(...  4.15 us
    all_to_all x1, starting transfers between devices, shards(): slots = lax.all_to_all(slots, ('gx', 'gy', 'gz'), 0, 0, tiled=True)  4.08 us
    pallas_call x1, Pallas kernels, shards(): pl.pallas_call(functools.partial(smooth_kernel, sizes), out_shape=(split,...  3.79 us
    all_to_all x1, waiting for transfers between devices, shards(): slots = lax.all_to_all(slots, ('gx', 'gy', 'gz'), 0, 0, tiled=True)  3.12 us
    pallas_call x1, Pallas kernels, shards(): pl.pallas_call(functools.partial(prepare_kernel, dims), out_shape=(shape(...  3.1 us
    pallas_call x1, Pallas kernels, shards(): pl.pallas_call(functools.partial(relax_kernel, sizes, dims), out_shape=sh...  1.47 us
  transfers between devices with their start and end apart: 4, of which 1 were waited for; matrix products, arithmetic and copies ran while one was open for 0% of the time, Pallas kernels for 23%

profile of v7, /device:TPU:0, one launch (start us, length us, event | category | flops | bytes accessed | tf_op | source)
XLA Modules:
  0.0 31.6 jit_solution(6924365802763654479)
XLA Ops:
  0.0 3.8 %smooth.1 = (bf16[512,512]{1,0:T(8,128)(2,1)S(1)}, bf16[512,512]{1,0:T(8,128)(2,1)S(1)}, bf16[512,512]{1,0:T(8,128)(2,1)S(1)}, bf16[512,512]{1,0:T(8,128)(2,1)S(...) custom-call(f32[512,512]{1,0:T(8,128)} %bitcast.3, ...), custom_call_target="tpu_custom_call" | custom-call | flops 2000000000 | bytes 4194304 | tf_op jit(solution)/shard_map/smooth/pallas_call | solution.py:537
  3.8 5.2 %all-to-all-start = ((f32[8,72,128]{2,1,0:T(8,128)}), f32[8,72,128]{2,1,0:T(8,128)S(1)}, u32[]{:S(2)}, u32[]{:S(2)}) async-start(f32[8,72,128]{2,1,0:T(8,128)} %get-tuple-element.34), calls=%async_computation | async-start | bytes 589824 | tf_op jit(solution)/shard_map/all_to_all | solution.py:576
  9.0 0.6 %collective-permute-start = (f32[16,128]{1,0:T(8,128)S(1)}, f32[16,128]{1,0:T(8,128)S(1)}, u32[]{:S(2)}, u32[]{:S(2)}) collective-permute-start(f32[16,128]{1,0:T(8,128)S(1)} %get-tuple-element.35), channel_id=1, source_target_pairs={{1,2},{2,1},{5,6},{6,5},{9,10},{10,9},{13,14},{14,13},{17,18},{18,... | collective-permute-start | bytes 24584 | tf_op jit(solution)/shard_map/ppermute | solution.py:574
  9.7 4.5 %collective-permute-start.1 = (f32[16,128]{1,0:T(8,128)S(1)}, f32[16,128]{1,0:T(8,128)S(1)}, u32[]{:S(2)}, u32[]{:S(2)}) collective-permute-start(f32[16,128]{1,0:T(8,128)S(1)} %get-tuple-element.36), channel_id=1, source_target_pairs={{0,1},{2,3},{1,0},{3,2},{4,5},{6,7},{5,4},{7,6},{8,9},{10,11},{9,8... | collective-permute-start | bytes 24584 | tf_op jit(solution)/shard_map/ppermute | solution.py:575
  14.2 3.1 %prepare.1 = (f32[64,512]{1,0:T(8,128)S(1)}, f32[8,512]{1,0:T(8,128)S(1)}, bf16[64,384]{1,0:T(8,128)(2,1)S(1)}, bf16[64,384]{1,0:T(8,128)(2,1)S(1)}, f32[4,128]{1,0:T(4,128)S(1)}) custom-call(f32[384,512]{1,0:T(8,128)} %l_hbm.3, f32[512,512]{1,0:T(8,128)} %m_hbm.1, bf16[512,512]{1,0:T(8,128)(2,1)S(1)} %get-tuple-element.25.uh_ref, ...), custom_call_target="tpu_custom_call" | custom-call | flops 2000000000 | bytes 4194304 | tf_op jit(solution)/shard_map/prepare/pallas_call | solution.py:577
  17.3 0.0 collective-permute-done.z1_ref
  17.3 0.0 collective-permute-done.1.z2_ref
  17.3 0.0 all-to-all-done.xy_ref
  17.3 1.5 %relax.1 = f32[32,4,128]{2,1,0:T(4,128)} custom-call(f32[64,512]{1,0:T(8,128)S(1)} %get-tuple-element.38.p_ref, f32[8,512]{1,0:T(8,128)S(1)} %get-tuple-element.39.own_ref, bf16[64,384]{1,0:T(8,128)(2,1)S(1)} %get-tuple-element.40.qh_ref, bf16[64,384]{1,0:T(8,128)(2,1)S(1)} %get-tuple-element.41.ql_ref, f32[8,8]{1,0:T(8,128)S(1)} %get-tuple-element.42.c_ref, ...), custom_call_target="tpu_custom_call" | custom-call | flops 2000000000 | bytes 4194304 | tf_op jit(solution)/shard_map/relax/pallas_call | solution.py:591
  18.8 4.1 %all-to-all-start.1 = ((f32[32,4,128]{2,1,0:T(4,128)}), f32[32,4,128]{2,1,0:T(4,128)S(1)}, u32[]{:S(2)}, u32[]{:S(2)}) async-start(f32[32,4,128]{2,1,0:T(4,128)} %relax.1), calls=%async_computation.1 | async-start | bytes 131072 | tf_op jit(solution)/shard_map/all_to_all | solution.py:604
  22.9 4.1 %second.1 = (f32[512,512]{1,0:T(8,128)S(1)}, bf16[32,512]{1,0:T(8,128)(2,1)S(1)}, bf16[512,128]{1,0:T(8,128)(2,1)S(1)}) custom-call(f32[512,512]{1,0:T(8,128)} %bitcast.4, f32[512,512]{1,0:T(8,128)} %s_hbm.3, f32[384,512]{1,0:T(8,128)} %l_hbm.3, bf16[512,512]{1,0:T(8,128)(2,1)S(1)} %get-tuple-element.25.uh_ref, ...), custom_call_target="tpu_custom_call" | custom-call | flops 2000000000 | bytes 4194304 | tf_op jit(solution)/shard_map/second/pallas_call | solution.py:605
  27.0 3.1 %all-to-all-done.1.slots_ref = f32[32,4,128]{2,1,0:T(4,128)S(1)} async-done(((f32[32,4,128]{2,1,0:T(4,128)}), f32[32,4,128]{2,1,0:T(4,128)S(1)}, u32[]{:S(2)}, u32[]{:S(2)}) %all-to-all-start.1) | async-done | bytes 65568 | tf_op jit(solution)/shard_map/all_to_all | solution.py:604
  30.2 1.5 %correct.1 = f32[512,512]{1,0:T(8,128)} custom-call(f32[512,512]{1,0:T(8,128)S(1)} %get-tuple-element.37.second_ref, f32[32,4,128]{2,1,0:T(4,128)S(1)} %all-to-all-done.1.slots_ref, f32[16,128]{1,0:T(8,128)S(1)} %get-tuple-element.33.meta_ref, bf16[512,128]{1,0:T(8,128)(2,1)S(1)} %get-tuple-element.43.oh_ref, bf16[32,512]{1,0:T(8,128)(2,1)S(1)} %get-tuple-element.44.rs_ref), custom_call_target="tpu_custom_call" | custom-call | tf_op jit(solution)/shard_map/correct/pallas_call | solution.py:624
Async XLA Ops:
  3.8 13.5 %all-to-all-start = ((f32[8,72,128]{2,1,0:T(8,128)}), f32[8,72,128]{2,1,0:T(8,128)S(1)}, u32[]{:S(2)}, u32[]{:S(2)}) async-start(f32[8,72,128]{2,1,0:T(8,128)} %get-tuple-element.34), calls=%async_computation | async-start | bytes 589824 | tf_op jit(solution)/shard_map/all_to_all | solution.py:576
  9.0 8.2 %collective-permute-start = (f32[16,128]{1,0:T(8,128)S(1)}, f32[16,128]{1,0:T(8,128)S(1)}, u32[]{:S(2)}, u32[]{:S(2)}) collective-permute-start(f32[16,128]{1,0:T(8,128)S(1)} %get-tuple-element.35), channel_id=1, source_target_pairs={{1,2},{2,1},{5,6},{6,5},{9,10},{10,9},{13,14},{14,13},{17,18},{18,... | collective-permute-start | bytes 24584 | tf_op jit(solution)/shard_map/ppermute | solution.py:574
  9.7 7.6 %collective-permute-start.1 = (f32[16,128]{1,0:T(8,128)S(1)}, f32[16,128]{1,0:T(8,128)S(1)}, u32[]{:S(2)}, u32[]{:S(2)}) collective-permute-start(f32[16,128]{1,0:T(8,128)S(1)} %get-tuple-element.36), channel_id=1, source_target_pairs={{0,1},{2,3},{1,0},{3,2},{4,5},{6,7},{5,4},{7,6},{8,9},{10,11},{9,8... | collective-permute-start | bytes 24584 | tf_op jit(solution)/shard_map/ppermute | solution.py:575
  18.8 11.4 %all-to-all-start.1 = ((f32[32,4,128]{2,1,0:T(4,128)}), f32[32,4,128]{2,1,0:T(4,128)S(1)}, u32[]{:S(2)}, u32[]{:S(2)}) async-start(f32[32,4,128]{2,1,0:T(4,128)} %relax.1), calls=%async_computation.1 | async-start | bytes 131072 | tf_op jit(solution)/shard_map/all_to_all | solution.py:604

commit v8 on v7

--- a/solution.py
+++ b/solution.py
@@ -202,9 +202,8 @@
         pl.when(there)(out.start)
         outs.append((there, out))
 
-    wait(4, 2)
+    wait(4, 4)
     near = near_part(blocks[0])
-    wait(6, 2)
     t_ref[...] = dot3(halves(rhs_ref[:, blocks[0]]), near)
     wait(8, 4)
     near = near_part(blocks[1])

time: 32 us -> 32 us (level)
  no operation moved by 1% of the time
where the time goes in v8:
time: 32 us; the launch traced here: 31.7 us
  starting transfers between devices  14.4 us (45%)
  Pallas kernels  14 us (44%)
  waiting for transfers between devices  3.12 us (10%)
    all_to_all x1, starting transfers between devices, shards(): xy = lax.all_to_all(xy, ('gx', 'gy'), 0, 0, tiled=True)  5.25 us
    ppermute x1, starting transfers between devices, shards(): z2 = lax.ppermute(z2, 'gz', swaps(0))  4.46 us
    pallas_call x1, Pallas kernels, shards(): pl.pallas_call(functools.partial(second_kernel, sizes, dims), out_shape=(...  4.15 us
    all_to_all x1, starting transfers between devices, shards(): slots = lax.all_to_all(slots, ('gx', 'gy', 'gz'), 0, 0, tiled=True)  4.07 us
    pallas_call x1, Pallas kernels, shards(): pl.pallas_call(functools.partial(smooth_kernel, sizes), out_shape=(split,...  3.83 us
    all_to_all x1, waiting for transfers between devices, shards(): slots = lax.all_to_all(slots, ('gx', 'gy', 'gz'), 0, 0, tiled=True)  3.11 us
    pallas_call x1, Pallas kernels, shards(): pl.pallas_call(functools.partial(prepare_kernel, dims), out_shape=(shape(...  3.11 us
    pallas_call x1, Pallas kernels, shards(): pl.pallas_call(correct_kernel, out_shape=shape((DOFS, DOFS), F32), out_sp...  1.47 us
  transfers between devices with their start and end apart: 4, of which 1 were waited for; matrix products, arithmetic and copies ran while one was open for 0% of the time, Pallas kernels for 23%

profile of v8, /device:TPU:0, one launch (start us, length us, event | category | flops | bytes accessed | tf_op | source)
XLA Modules:
  0.0 31.7 jit_solution(6909776821264474529)
XLA Ops:
  0.0 3.8 %smooth.1 = (bf16[512,512]{1,0:T(8,128)(2,1)S(1)}, bf16[512,512]{1,0:T(8,128)(2,1)S(1)}, bf16[512,512]{1,0:T(8,128)(2,1)S(1)}, bf16[512,512]{1,0:T(8,128)(2,1)S(...) custom-call(f32[512,512]{1,0:T(8,128)} %bitcast.3, ...), custom_call_target="tpu_custom_call" | custom-call | flops 2000000000 | bytes 4194304 | tf_op jit(solution)/shard_map/smooth/pallas_call | solution.py:536
  3.8 5.3 %all-to-all-start = ((f32[8,72,128]{2,1,0:T(8,128)}), f32[8,72,128]{2,1,0:T(8,128)S(1)}, u32[]{:S(2)}, u32[]{:S(2)}) async-start(f32[8,72,128]{2,1,0:T(8,128)} %get-tuple-element.34), calls=%async_computation | async-start | bytes 589824 | tf_op jit(solution)/shard_map/all_to_all | solution.py:575
  9.1 0.6 %collective-permute-start = (f32[16,128]{1,0:T(8,128)S(1)}, f32[16,128]{1,0:T(8,128)S(1)}, u32[]{:S(2)}, u32[]{:S(2)}) collective-permute-start(f32[16,128]{1,0:T(8,128)S(1)} %get-tuple-element.35), channel_id=1, source_target_pairs={{1,2},{2,1},{5,6},{6,5},{9,10},{10,9},{13,14},{14,13},{17,18},{18,... | collective-permute-start | bytes 24584 | tf_op jit(solution)/shard_map/ppermute | solution.py:573
  9.7 4.5 %collective-permute-start.1 = (f32[16,128]{1,0:T(8,128)S(1)}, f32[16,128]{1,0:T(8,128)S(1)}, u32[]{:S(2)}, u32[]{:S(2)}) collective-permute-start(f32[16,128]{1,0:T(8,128)S(1)} %get-tuple-element.36), channel_id=1, source_target_pairs={{0,1},{2,3},{1,0},{3,2},{4,5},{6,7},{5,4},{7,6},{8,9},{10,11},{9,8... | collective-permute-start | bytes 24584 | tf_op jit(solution)/shard_map/ppermute | solution.py:574
  14.2 3.1 %prepare.1 = (f32[64,512]{1,0:T(8,128)S(1)}, f32[8,512]{1,0:T(8,128)S(1)}, bf16[64,384]{1,0:T(8,128)(2,1)S(1)}, bf16[64,384]{1,0:T(8,128)(2,1)S(1)}, f32[4,128]{1,0:T(4,128)S(1)}) custom-call(f32[384,512]{1,0:T(8,128)} %l_hbm.3, f32[512,512]{1,0:T(8,128)} %m_hbm.1, bf16[512,512]{1,0:T(8,128)(2,1)S(1)} %get-tuple-element.25.uh_ref, ...), custom_call_target="tpu_custom_call" | custom-call | flops 2000000000 | bytes 4194304 | tf_op jit(solution)/shard_map/prepare/pallas_call | solution.py:576
  17.3 0.0 collective-permute-done.z1_ref
  17.3 0.0 collective-permute-done.1.z2_ref
  17.4 0.0 all-to-all-done.xy_ref
  17.4 1.5 %relax.1 = f32[32,4,128]{2,1,0:T(4,128)} custom-call(f32[64,512]{1,0:T(8,128)S(1)} %get-tuple-element.38.p_ref, f32[8,512]{1,0:T(8,128)S(1)} %get-tuple-element.39.own_ref, bf16[64,384]{1,0:T(8,128)(2,1)S(1)} %get-tuple-element.40.qh_ref, bf16[64,384]{1,0:T(8,128)(2,1)S(1)} %get-tuple-element.41.ql_ref, f32[8,8]{1,0:T(8,128)S(1)} %get-tuple-element.42.c_ref, ...), custom_call_target="tpu_custom_call" | custom-call | flops 2000000000 | bytes 4194304 | tf_op jit(solution)/shard_map/relax/pallas_call | solution.py:590
  18.8 4.1 %all-to-all-start.1 = ((f32[32,4,128]{2,1,0:T(4,128)}), f32[32,4,128]{2,1,0:T(4,128)S(1)}, u32[]{:S(2)}, u32[]{:S(2)}) async-start(f32[32,4,128]{2,1,0:T(4,128)} %relax.1), calls=%async_computation.1 | async-start | bytes 131072 | tf_op jit(solution)/shard_map/all_to_all | solution.py:603
  22.9 4.2 %second.1 = (f32[512,512]{1,0:T(8,128)S(1)}, bf16[32,512]{1,0:T(8,128)(2,1)S(1)}, bf16[512,128]{1,0:T(8,128)(2,1)S(1)}) custom-call(f32[512,512]{1,0:T(8,128)} %bitcast.4, f32[512,512]{1,0:T(8,128)} %s_hbm.3, f32[384,512]{1,0:T(8,128)} %l_hbm.3, bf16[512,512]{1,0:T(8,128)(2,1)S(1)} %get-tuple-element.25.uh_ref, ...), custom_call_target="tpu_custom_call" | custom-call | flops 2000000000 | bytes 4194304 | tf_op jit(solution)/shard_map/second/pallas_call | solution.py:604
  27.1 3.1 %all-to-all-done.1.slots_ref = f32[32,4,128]{2,1,0:T(4,128)S(1)} async-done(((f32[32,4,128]{2,1,0:T(4,128)}), f32[32,4,128]{2,1,0:T(4,128)S(1)}, u32[]{:S(2)}, u32[]{:S(2)}) %all-to-all-start.1) | async-done | bytes 65568 | tf_op jit(solution)/shard_map/all_to_all | solution.py:603
  30.2 1.5 %correct.1 = f32[512,512]{1,0:T(8,128)} custom-call(f32[512,512]{1,0:T(8,128)S(1)} %get-tuple-element.37.second_ref, f32[32,4,128]{2,1,0:T(4,128)S(1)} %all-to-all-done.1.slots_ref, f32[16,128]{1,0:T(8,128)S(1)} %get-tuple-element.33.meta_ref, bf16[512,128]{1,0:T(8,128)(2,1)S(1)} %get-tuple-element.43.oh_ref, bf16[32,512]{1,0:T(8,128)(2,1)S(1)} %get-tuple-element.44.rs_ref), custom_call_target="tpu_custom_call" | custom-call | tf_op jit(solution)/shard_map/correct/pallas_call | solution.py:623
Async XLA Ops:
  3.8 13.5 %all-to-all-start = ((f32[8,72,128]{2,1,0:T(8,128)}), f32[8,72,128]{2,1,0:T(8,128)S(1)}, u32[]{:S(2)}, u32[]{:S(2)}) async-start(f32[8,72,128]{2,1,0:T(8,128)} %get-tuple-element.34), calls=%async_computation | async-start | bytes 589824 | tf_op jit(solution)/shard_map/all_to_all | solution.py:575
  9.1 8.2 %collective-permute-start = (f32[16,128]{1,0:T(8,128)S(1)}, f32[16,128]{1,0:T(8,128)S(1)}, u32[]{:S(2)}, u32[]{:S(2)}) collective-permute-start(f32[16,128]{1,0:T(8,128)S(1)} %get-tuple-element.35), channel_id=1, source_target_pairs={{1,2},{2,1},{5,6},{6,5},{9,10},{10,9},{13,14},{14,13},{17,18},{18,... | collective-permute-start | bytes 24584 | tf_op jit(solution)/shard_map/ppermute | solution.py:573
  9.7 7.6 %collective-permute-start.1 = (f32[16,128]{1,0:T(8,128)S(1)}, f32[16,128]{1,0:T(8,128)S(1)}, u32[]{:S(2)}, u32[]{:S(2)}) collective-permute-start(f32[16,128]{1,0:T(8,128)S(1)} %get-tuple-element.36), channel_id=1, source_target_pairs={{0,1},{2,3},{1,0},{3,2},{4,5},{6,7},{5,4},{7,6},{8,9},{10,11},{9,8... | collective-permute-start | bytes 24584 | tf_op jit(solution)/shard_map/ppermute | solution.py:574
  18.8 11.4 %all-to-all-start.1 = ((f32[32,4,128]{2,1,0:T(4,128)}), f32[32,4,128]{2,1,0:T(4,128)S(1)}, u32[]{:S(2)}, u32[]{:S(2)}) async-start(f32[32,4,128]{2,1,0:T(4,128)} %relax.1), calls=%async_computation.1 | async-start | bytes 131072 | tf_op jit(solution)/shard_map/all_to_all | solution.py:603
